TPU v7x, 32 devices: a whole 2x2x4 slice. The times are simulated.
32 devices in a mesh: grp: 2 (over y), rot: 4 (over z), shell: 2 (over x), ang: 2 (over core).
Axes of the slice: x: 2, y: 2, z: 4, core: 2. Of those that a mesh axis runs over, the one named last changes fastest.
Arguments:
- images: float32 [2, 128, 64, 2048], P(None, 'shell', 'ang', ('grp', 'rot')), parts along dimension 3, may hold values from -16 to 16
- references: bfloat16 [2, 128, 64, 2048], P(None, 'shell', 'ang', ('grp', 'rot')), parts along dimension 3, may hold values from -4 to 4
- noise_weight: float32 [256], P(('grp', 'shell')), parts along dimension 0, may hold values from 0.004 to 0.03
- euler_angles: float32 [3, 2048], P(None, ('grp', 'rot')), parts along dimension 1, may hold values from -3.140625 to 3.140625
- candidate_count: int32 [16, 4], P(('grp', 'rot')), parts along dimension 0, may hold values from 0 to 8, as said below
- candidate_rotation: int32 [16, 4, 8], P(('grp', 'rot')), parts along dimension 0, may hold values from 0 to 255, as said below
- image_order: int32 [2048], P(('grp', 'rot')), parts along dimension 0, may hold values from 0 to 255, as said below
Outputs:
- coefficients: float32 [2048, 2, 128], P(('grp', 'rot', 'ang'), None, 'shell'), parts along dimension 0
- log_evidence: float32 [2048], P(('grp', 'rot')), parts along dimension 0
There are 2 independent parts, one for each index of `grp`. A program takes and returns all parts, laid end to end along the dimension named above; each array names one. Nothing has to cross between parts.
Inputs may be any that keep to these rules, and one draw needn't show every extreme that they name: `image_order`: within each device's 256 entries, a permutation of 0 to 255. `candidate_count`: for the 2 blocks of one device and one owner the counts add up to at most 8; in every draw one owner, drawn from the seed, gets exactly 8 from every device, with 8 in one block of each device; every block has two or more candidates in all. `candidate_rotation`: the 8 entries of one block and owner are distinct; entries at or past the count are not used.
All inputs are finite; a program needn't handle non-finite values.
Results may differ from a plain program's by a relative error of at most 0.0074.
Values may be sent and summed in bfloat16 or wider, within the bound.
A program may use at most 64 MiB of HBM per device.

v0:
```python
import math

import jax
import jax.numpy as jnp
from jax import lax
from jax.sharding import PartitionSpec as P

ANGLES = 64
ORDER = 32
BLOCK = 128
CPO = 8
COEF = 1024


angle_step = 8


def legendre_constants(degrees):
    first_coef = []
    second_coef = []
    for degree in range(degrees):
        first_line = []
        second_line = []
        for azimuth in range(degrees):
            if azimuth < degree:
                first_line.append(
                    math.sqrt((4.0 * degree * degree - 1.0) / (degree * degree - azimuth * azimuth))
                )
                lower_term = max((degree - 1.0) ** 2 - azimuth * azimuth, 0.0)
                lower_den = max(4.0 * (degree - 1.0) ** 2 - 1.0, 1.0)
                second_line.append(math.sqrt(lower_term / lower_den))
            else:
                first_line.append(0.0)
                second_line.append(0.0)
        first_coef.append(first_line)
        second_coef.append(second_line)
    diagonal = []
    running = 1.0
    for degree in range(degrees):
        if degree > 0:
            running = running * (2.0 * degree - 1.0) / (2.0 * degree)
        diagonal.append(math.sqrt((2.0 * degree + 1.0) / (4.0 * math.pi) * running))
    pick_rows = []
    pick_trig = []
    factors = []
    for degree in range(degrees):
        pick_rows.append(degree * degrees)
        pick_trig.append(0)
        factors.append(1.0)
        for azimuth in range(1, degree + 1):
            for parity in range(2):
                pick_rows.append(degree * degrees + azimuth)
                pick_trig.append(parity * degrees + azimuth)
                factors.append(math.sqrt(2.0))
    return (first_coef, second_coef, diagonal, pick_rows, pick_trig, factors)


def harmonic_table(euler_angles, angle_ids, angle_count, degrees):
    first_coef, second_coef, diagonal, pick_rows, pick_trig, factors = legendre_constants(degrees)
    in_plane = 2.0 * math.pi / angle_count * angle_ids.astype(jnp.float32)
    phases = in_plane[:, None] + euler_angles[2][None, :]
    cos_phase = jnp.cos(phases)
    sin_phase = jnp.sin(phases)
    cos_alpha = jnp.cos(euler_angles[0])[None, :]
    sin_alpha = jnp.sin(euler_angles[0])[None, :]
    cos_beta = jnp.cos(euler_angles[1])[None, :]
    sin_beta = jnp.sin(euler_angles[1])[None, :]
    along_x = (cos_alpha * cos_beta * cos_phase - sin_alpha * sin_phase).reshape(-1)
    along_y = (sin_alpha * cos_beta * cos_phase + cos_alpha * sin_phase).reshape(-1)
    along_z = (-sin_beta * cos_phase).reshape(-1)

    def trig_step(carry, unused):
        real_part, imag_part = carry
        return (
            (along_x * real_part - along_y * imag_part, along_x * imag_part + along_y * real_part),
            carry,
        )

    unused_carry, (real_rows, imag_rows) = lax.scan(
        trig_step, (jnp.ones_like(along_x), jnp.zeros_like(along_x)), None, length=degrees
    )
    azimuths = jnp.arange(degrees)
    diag_col = jnp.asarray(diagonal, jnp.float32)[:, None]

    def legendre_step(carry, inputs):
        previous, earlier = carry
        degree, coef_first, coef_second = inputs
        current = coef_first[:, None] * (
            along_z[None, :] * previous - coef_second[:, None] * earlier
        )
        current = jnp.where((azimuths == degree)[:, None], diag_col, current)
        return ((current, previous), current)

    zero_rows = jnp.zeros((degrees, along_z.shape[0]), jnp.float32)
    unused_state, stacked = lax.scan(
        legendre_step,
        (zero_rows, zero_rows),
        (
            jnp.arange(degrees),
            jnp.asarray(first_coef, jnp.float32),
            jnp.asarray(second_coef, jnp.float32),
        ),
    )
    legendre = stacked.reshape(degrees * degrees, -1)
    trig_rows = jnp.concatenate([real_rows, imag_rows], axis=0)
    table_rows = (
        jnp.take(legendre, jnp.asarray(pick_rows, jnp.int32), axis=0)
        * jnp.take(trig_rows, jnp.asarray(pick_trig, jnp.int32), axis=0)
        * jnp.asarray(factors, jnp.float32)[:, None]
    )
    return table_rows.astype(jnp.bfloat16)


def per_device(
    images, references, noise_weight, euler_angles, candidate_count, candidate_rotation, image_order
):
    owners = lax.axis_size("rot")
    shells_here = images.shape[1]
    angles_here = images.shape[2]
    features = 2 * shells_here * angles_here
    rotations_here = references.shape[3]
    blocks_here = candidate_count.shape[0]
    shell_scale = jnp.broadcast_to(
        noise_weight[None, :, None], (2, shells_here, angles_here)
    ).reshape(features)
    weighted = (images.reshape(features, -1) * shell_scale[:, None]).astype(jnp.bfloat16)
    members = jnp.take(weighted, image_order, axis=1).reshape(features, blocks_here, BLOCK)
    slice_table = references.reshape(features, rotations_here)
    rotation_ids = jnp.arange(rotations_here)
    slot_ids = jnp.arange(CPO)
    slot_valid = slot_ids[None, None, :] < candidate_count[:, :, None]
    requests = lax.all_to_all(candidate_rotation, "rot", split_axis=1, concat_axis=1, tiled=True)
    wanted = jnp.transpose(requests, (1, 0, 2)).reshape(-1)
    selector = (rotation_ids[:, None] == wanted[None, :]).astype(jnp.bfloat16)
    picked = lax.dot_general(
        selector, slice_table, (((0,), (1,)), ((), ())), preferred_element_type=jnp.float32
    ).astype(jnp.bfloat16)
    slices = lax.all_to_all(
        picked.reshape(owners, blocks_here * CPO, features),
        "rot",
        split_axis=0,
        concat_axis=0,
        tiled=True,
    )
    slices = slices.reshape(owners, blocks_here, CPO, features)
    slot_norms = jnp.sum(jnp.square(slices.astype(jnp.float32)) * shell_scale, axis=3)
    products = jnp.einsum("fbi,objf->bioj", members, slices, preferred_element_type=jnp.float32)
    partial_scores = 2.0 * products - jnp.transpose(slot_norms, (1, 0, 2))[:, None]
    scores = lax.psum(partial_scores, ("shell", "ang"))
    masked = jnp.where(slot_valid[:, None], scores, -jnp.inf)
    highest = jnp.max(masked, axis=(2, 3))
    totals = jnp.sum(jnp.exp(masked - highest[:, :, None, None]), axis=(2, 3))
    evidence = highest + jnp.log(totals)
    weights = jnp.exp(masked - evidence[:, :, None, None]).astype(jnp.bfloat16)
    log_evidence = (
        jnp.zeros(image_order.shape, jnp.float32).at[image_order].set(evidence.reshape(-1))
    )
    averages = jnp.einsum(
        "bioj,fbi->objf", weights, members, preferred_element_type=jnp.float32
    ).astype(jnp.bfloat16)
    returned = lax.all_to_all(
        averages.reshape(owners, blocks_here * CPO, features),
        "rot",
        split_axis=0,
        concat_axis=0,
        tiled=True,
    )
    summed = lax.dot_general(
        returned.reshape(-1, features),
        selector,
        (((0,), (1,)), ((), ())),
        preferred_element_type=jnp.float32,
    )
    rotation_average = summed.astype(jnp.bfloat16).reshape(
        2 * shells_here, angles_here, rotations_here
    )
    angle_base = lax.axis_index("ang") * angles_here

    def add_angles(turn_id, running_sum):
        angle_plane = lax.dynamic_slice_in_dim(
            rotation_average, turn_id * angle_step, angle_step, 1
        ).reshape(2 * shells_here, -1)
        angle_ids = angle_base + turn_id * angle_step + jnp.arange(angle_step)
        harmonics = harmonic_table(euler_angles, angle_ids, ANGLES, ORDER)
        return running_sum + lax.dot_general(
            harmonics, angle_plane, (((1,), (1,)), ((), ())), preferred_element_type=jnp.float32
        )

    partial_coef = lax.fori_loop(
        0, angles_here // angle_step, add_angles, jnp.zeros((COEF, 2 * shells_here), jnp.float32)
    )
    grouped = partial_coef.reshape(owners, lax.axis_size("ang"), -1, 2 * shells_here)
    grouped = lax.psum_scatter(grouped, "ang", scatter_dimension=1, tiled=True)
    coefficients = lax.psum_scatter(grouped, "rot", scatter_dimension=0, tiled=True)
    return (coefficients.reshape(-1, 2, shells_here), log_evidence)


def solution(mesh):
    in_specs = (
        P(None, "shell", "ang", ("grp", "rot")),
        P(None, "shell", "ang", ("grp", "rot")),
        P(("grp", "shell")),
        P(None, ("grp", "rot")),
        P(("grp", "rot"), None),
        P(("grp", "rot"), None, None),
        P(("grp", "rot")),
    )
    out_specs = (P(("grp", "rot", "ang"), None, "shell"), P(("grp", "rot")))
    return jax.shard_map(
        per_device, mesh=mesh, in_specs=in_specs, out_specs=out_specs, check_vma=False
    )
```

profile of v0, /device:TPU:0, one launch (start us, length us, event | category | flops | bytes accessed | tf_op | source)
XLA Modules:
  0.0 699.0 jit_solution(7712533928371600952)
XLA Ops:
  8.6 6.3 all-to-all-start
  14.9 5.6 copy.33
  22.4 5.2 all-to-all-start.1
  27.6 3.9 multiply_convert_fusion.4
  31.5 7.1 %gather_fusion.2 = bf16[256,4096]{1,0:T(8,128)(2,1)} fusion(bf16[4096,256]{0,1:T(8,128)(2,1)} %multiply_convert_fusion.4, s32[1024]{0:T(1024)S(1)} %pad_clamp_fusion), kind=kCustom, calls=%fused_computation.2 | custom fusion | bytes 4195328 | tf_op jit(solution)/shard_map/jit(_take)/gather | solution.py:127
  38.6 4.1 copy.34
  45.2 10.3 %psum.7 = f32[2,128,4,8]{1,3,2,0:T(8,128)S(1)} all-reduce(f32[2,128,4,8]{1,3,2,0:T(8,128)S(1)} %fusion.28), channel_id=1, replica_groups=mesh['grp'=2,'rot'=4,'shell'=2,'ang'=2] {'shell','ang'}, use_global_device_ids=true, to_apply=%region_1.2 | all-reduce | flops 8192 | bytes 65536 | tf_op jit(solution)/shard_map/psum | solution.py:149
  59.1 5.1 all-to-all-start.2
  64.3 14.7 %all-to-all-done.2 = bf16[4,16,4096]{2,1,0:T(8,128)(2,1)S(1)} async-done(((bf16[4,16,4096]{2,1,0:T(8,128)(2,1)}), bf16[4,16,4096]{2,1,0:T(8,128)(2,1)S(1)}, u32[]{:S(2)}, u32[]{:S(2)}) %all-to-all-start.2) | async-done | bytes 524320 | tf_op jit(solution)/shard_map/all_to_all | solution.py:161
  81.0 567.7 %while.109 = (s32[]{:T(128)}, f32[1024,128]{1,0:T(8,128)}, f32[1,256]{1,0:T(1,128)S(1)}, s32[]{:T(128)}, f32[3,256]{1,0:T(4,128)S(1)}, /*index=5*/f32[1,256]{1,0...) while((s32[]{:T(128)}, f32[1024,128]{1,0:T(8,128)}, ...), condition=%wide.region_9.10_spmd.clone.clone, body=%wide.region_4.9_spmd.sunk.clone.clone.sunk | while | flops 543985728 | bytes 58449052 | solution.py:189
  82.3 91.6 %while.110 = (s32[]{:T(128)}, f32[32,2048]{1,0:T(8,128)S(1)}, f32[32,2048]{1,0:T(8,128)S(1)}, f32[32,32,2048]{2,1,0:T(8,128)}, s32[32]{0:T(128)S(1)}, /*index=5*...) while((s32[]{:T(128)}, f32[32,2048]{1,0:T(8,128)S(1)}, ...), condition=%wide.region_6.6_spmd.clone.clone.clone.clone.clone, body=%wide.region_5.5_spmd.sunk.clone.clone.clone.clone.clone.sunk | while | flops 397347 | bytes 1346823 | solution.py:95
  173.9 12.4 %gather_fusion = f32[1024,2048]{1,0:T(8,128)} fusion(f32[1024,2048]{1,0:T(8,128)} %bitcast.135, s32[1024]{0:T(1024)S(1)} %broadcast_clamp_fusion.4), kind=kCustom, calls=%fused_computation.clone.clone.1 | custom fusion | bytes 16781312 | tf_op jit(solution)/shard_map/while/body/eval_jaxpr/jit(_take)/gather | solution.py:107
  186.3 20.1 %while.111 = (s32[]{:T(128)}, f32[2048]{0:T(1024)S(1)}, f32[2048]{0:T(1024)S(1)}, f32[32,2048]{1,0:T(8,128)S(1)}, f32[32,2048]{1,0:T(8,128)S(1)}, /*index=5*/f32...) while((s32[]{:T(128)}, f32[2048]{0:T(1024)S(1)}, ...), condition=%wide.region_8.8_spmd.clone.clone.clone, body=%wide.region_7.7_spmd.clone.clone.clone.sunk | while | flops 30723 | bytes 185527 | solution.py:79
  208.2 6.9 gather_fusion.1
  215.0 7.9 %fusion.59 = f32[1024,128]{1,0:T(8,128)} fusion(bf16[128,2048]{1,0:T(8,128)(2,1)S(1)} %bitcast.136, f32[1024,2048]{1,0:T(8,128)} %gather_fusion, f32[1024,2048]{1,0:T(8,128)} %gather_fusion.1, f32[1024]{0:T(1024)S(1)} %get-tuple-element.1286, f32[1024,128]{1,0:T(8,128)} %get-tuple-element.1238, pred[]{:T(512)S(6)} %compare.13), kind=kOutput, calls=%fused_computation.34.clone.1 | convolution fusion | flops 543424512 | bytes 18354176 | tf_op jit(solution)/shard_map/while/body/eval_jaxpr/dot_general | solution.py:185
  224.2 91.6 %while.110 = (s32[]{:T(128)}, f32[32,2048]{1,0:T(8,128)S(1)}, f32[32,2048]{1,0:T(8,128)S(1)}, f32[32,32,2048]{2,1,0:T(8,128)}, s32[32]{0:T(128)S(1)}, /*index=5*...) while((s32[]{:T(128)}, f32[32,2048]{1,0:T(8,128)S(1)}, ...), condition=%wide.region_6.6_spmd.clone.clone.clone.clone.clone, body=%wide.region_5.5_spmd.sunk.clone.clone.clone.clone.clone.sunk | while | flops 397347 | bytes 1346823 | solution.py:95
  315.8 12.4 %gather_fusion = f32[1024,2048]{1,0:T(8,128)} fusion(f32[1024,2048]{1,0:T(8,128)} %bitcast.135, s32[1024]{0:T(1024)S(1)} %broadcast_clamp_fusion.4), kind=kCustom, calls=%fused_computation.clone.clone.1 | custom fusion | bytes 16781312 | tf_op jit(solution)/shard_map/while/body/eval_jaxpr/jit(_take)/gather | solution.py:107
  328.2 20.1 %while.111 = (s32[]{:T(128)}, f32[2048]{0:T(1024)S(1)}, f32[2048]{0:T(1024)S(1)}, f32[32,2048]{1,0:T(8,128)S(1)}, f32[32,2048]{1,0:T(8,128)S(1)}, /*index=5*/f32...) while((s32[]{:T(128)}, f32[2048]{0:T(1024)S(1)}, ...), condition=%wide.region_8.8_spmd.clone.clone.clone, body=%wide.region_7.7_spmd.clone.clone.clone.sunk | while | flops 30723 | bytes 185527 | solution.py:79
  350.0 6.9 gather_fusion.1
  356.9 7.9 %fusion.59 = f32[1024,128]{1,0:T(8,128)} fusion(bf16[128,2048]{1,0:T(8,128)(2,1)S(1)} %bitcast.136, f32[1024,2048]{1,0:T(8,128)} %gather_fusion, f32[1024,2048]{1,0:T(8,128)} %gather_fusion.1, f32[1024]{0:T(1024)S(1)} %get-tuple-element.1286, f32[1024,128]{1,0:T(8,128)} %get-tuple-element.1238, pred[]{:T(512)S(6)} %compare.13), kind=kOutput, calls=%fused_computation.34.clone.1 | convolution fusion | flops 543424512 | bytes 18354176 | tf_op jit(solution)/shard_map/while/body/eval_jaxpr/dot_general | solution.py:185
  366.1 91.6 %while.110 = (s32[]{:T(128)}, f32[32,2048]{1,0:T(8,128)S(1)}, f32[32,2048]{1,0:T(8,128)S(1)}, f32[32,32,2048]{2,1,0:T(8,128)}, s32[32]{0:T(128)S(1)}, /*index=5*...) while((s32[]{:T(128)}, f32[32,2048]{1,0:T(8,128)S(1)}, ...), condition=%wide.region_6.6_spmd.clone.clone.clone.clone.clone, body=%wide.region_5.5_spmd.sunk.clone.clone.clone.clone.clone.sunk | while | flops 397347 | bytes 1346823 | solution.py:95
  457.7 12.4 %gather_fusion = f32[1024,2048]{1,0:T(8,128)} fusion(f32[1024,2048]{1,0:T(8,128)} %bitcast.135, s32[1024]{0:T(1024)S(1)} %broadcast_clamp_fusion.4), kind=kCustom, calls=%fused_computation.clone.clone.1 | custom fusion | bytes 16781312 | tf_op jit(solution)/shard_map/while/body/eval_jaxpr/jit(_take)/gather | solution.py:107
  470.1 20.1 %while.111 = (s32[]{:T(128)}, f32[2048]{0:T(1024)S(1)}, f32[2048]{0:T(1024)S(1)}, f32[32,2048]{1,0:T(8,128)S(1)}, f32[32,2048]{1,0:T(8,128)S(1)}, /*index=5*/f32...) while((s32[]{:T(128)}, f32[2048]{0:T(1024)S(1)}, ...), condition=%wide.region_8.8_spmd.clone.clone.clone, body=%wide.region_7.7_spmd.clone.clone.clone.sunk | while | flops 30723 | bytes 185527 | solution.py:79
  491.9 6.9 gather_fusion.1
  498.8 7.9 %fusion.59 = f32[1024,128]{1,0:T(8,128)} fusion(bf16[128,2048]{1,0:T(8,128)(2,1)S(1)} %bitcast.136, f32[1024,2048]{1,0:T(8,128)} %gather_fusion, f32[1024,2048]{1,0:T(8,128)} %gather_fusion.1, f32[1024]{0:T(1024)S(1)} %get-tuple-element.1286, f32[1024,128]{1,0:T(8,128)} %get-tuple-element.1238, pred[]{:T(512)S(6)} %compare.13), kind=kOutput, calls=%fused_computation.34.clone.1 | convolution fusion | flops 543424512 | bytes 18354176 | tf_op jit(solution)/shard_map/while/body/eval_jaxpr/dot_general | solution.py:185
  508.1 91.6 %while.110 = (s32[]{:T(128)}, f32[32,2048]{1,0:T(8,128)S(1)}, f32[32,2048]{1,0:T(8,128)S(1)}, f32[32,32,2048]{2,1,0:T(8,128)}, s32[32]{0:T(128)S(1)}, /*index=5*...) while((s32[]{:T(128)}, f32[32,2048]{1,0:T(8,128)S(1)}, ...), condition=%wide.region_6.6_spmd.clone.clone.clone.clone.clone, body=%wide.region_5.5_spmd.sunk.clone.clone.clone.clone.clone.sunk | while | flops 397347 | bytes 1346823 | solution.py:95
  599.6 12.4 %gather_fusion = f32[1024,2048]{1,0:T(8,128)} fusion(f32[1024,2048]{1,0:T(8,128)} %bitcast.135, s32[1024]{0:T(1024)S(1)} %broadcast_clamp_fusion.4), kind=kCustom, calls=%fused_computation.clone.clone.1 | custom fusion | bytes 16781312 | tf_op jit(solution)/shard_map/while/body/eval_jaxpr/jit(_take)/gather | solution.py:107
  612.1 20.1 %while.111 = (s32[]{:T(128)}, f32[2048]{0:T(1024)S(1)}, f32[2048]{0:T(1024)S(1)}, f32[32,2048]{1,0:T(8,128)S(1)}, f32[32,2048]{1,0:T(8,128)S(1)}, /*index=5*/f32...) while((s32[]{:T(128)}, f32[2048]{0:T(1024)S(1)}, ...), condition=%wide.region_8.8_spmd.clone.clone.clone, body=%wide.region_7.7_spmd.clone.clone.clone.sunk | while | flops 30723 | bytes 185527 | solution.py:79
  633.9 6.9 gather_fusion.1
  640.8 7.9 %fusion.59 = f32[1024,128]{1,0:T(8,128)} fusion(bf16[128,2048]{1,0:T(8,128)(2,1)S(1)} %bitcast.136, f32[1024,2048]{1,0:T(8,128)} %gather_fusion, f32[1024,2048]{1,0:T(8,128)} %gather_fusion.1, f32[1024]{0:T(1024)S(1)} %get-tuple-element.1286, f32[1024,128]{1,0:T(8,128)} %get-tuple-element.1238, pred[]{:T(512)S(6)} %compare.13), kind=kOutput, calls=%fused_computation.34.clone.1 | convolution fusion | flops 543424512 | bytes 18354176 | tf_op jit(solution)/shard_map/while/body/eval_jaxpr/dot_general | solution.py:185
  651.4 17.0 %all-reduce.3.cloned.1.call-done = f32[4,2,128,128]{2,3,1,0:T(8,128)} async-done(((f32[4,2,128,128]{2,3,1,0:T(8,128)}), f32[4,2,128,128]{2,3,1,0:T(8,128)}) %all-reduce.3.cloned.1.call-update) | async-done | bytes 524304
  672.8 19.4 %reduce-scatter.5.cloned.1.call-done = f32[1,1,128,128]{2,3,1,0:T(8,128)} async-done(((f32[4,1,128,128]{2,3,1,0:T(8,128)}), f32[1,1,128,128]{2,3,1,0:T(8,128)}) %reduce-scatter.5.cloned.1.call-update) | async-done | bytes 65552 | tf_op jit(solution)/shard_map/reduce_scatter | solution.py:194
  (1787 shorter events, 465.4 us)
Async XLA Ops:
  7.2 13.7 %copy-start = (bf16[2,64,32,256]{3,2,1,0:T(8,128)(2,1)S(1)}, bf16[2,64,32,256]{3,2,1,0:T(8,128)(2,1)}, u32[]{:S(2)}) copy-start(bf16[2,64,32,256]{3,2,1,0:T(8,128)(2,1)} %param.20) | copy-start | bytes 6291460
  8.6 12.1 %all-to-all-start = ((s32[2,4,8]{2,0,1:T(2,128)}), s32[2,4,8]{2,0,1:T(2,128)S(1)}, u32[]{:S(2)}, u32[]{:S(2)}) async-start(s32[2,4,8]{2,0,1:T(2,128)} %copy.35), calls=%async_computation | async-start | bytes 8192 | tf_op jit(solution)/shard_map/all_to_all | solution.py:132
  14.9 5.6 copy-start.11
  22.4 9.1 %copy-start.9 = (s32[256]{0:T(256)S(1)}, s32[256]{0:T(256)}, u32[]{:S(2)}) copy-start(s32[256]{0:T(256)} %param.25) | copy-start | bytes 3076
  22.4 20.4 %all-to-all-start.1 = ((bf16[4,16,4096]{2,1,0:T(8,128)(2,1)}), bf16[4,16,4096]{2,1,0:T(8,128)(2,1)S(1)}, u32[]{:S(2)}, u32[]{:S(2)}) async-start(bf16[4,16,4096]{2,1,0:T(8,128)(2,1)} %bitcast.8), calls=%async_computation.1 | async-start | bytes 1048576 | tf_op jit(solution)/shard_map/all_to_all | solution.py:138
  31.5 7.1 %copy-start.7 = (s32[256]{0:T(256)}, s32[256]{0:T(256)S(1)}, u32[]{:S(2)}) copy-start(s32[256]{0:T(256)S(1)} %compare_select_fusion) | copy-start | bytes 3076
  38.6 4.1 copy-start.10
  45.2 19.0 %copy-start.6 = (f32[3,256]{1,0:T(4,128)S(1)}, f32[3,256]{1,0:T(4,128)}, u32[]{:S(2)}) copy-start(f32[3,256]{1,0:T(4,128)} %param.22) | copy-start | bytes 9220
  55.7 3.4 copy-start.8
  55.7 25.3 %copy-start.2 = (f32[32]{0:T(128)S(1)}, f32[32]{0:T(128)}, u32[]{:S(2)}) copy-start(f32[32]{0:T(128)} %constant.312) | copy-start | bytes 388
  55.7 25.3 %copy-start.3 = (f32[1024]{0:T(1024)S(1)}, f32[1024]{0:T(1024)}, u32[]{:S(2)}) copy-start(f32[1024]{0:T(1024)} %constant.210.clone..sunk.3) | copy-start | bytes 12292
  55.7 25.3 %copy-start.4 = (s32[1024]{0:T(1024)S(1)}, s32[1024]{0:T(1024)}, u32[]{:S(2)}) copy-start(s32[1024]{0:T(1024)} %constant.313) | copy-start | bytes 12292
  55.8 25.3 %copy-start.5 = (s32[1024]{0:T(1024)S(1)}, s32[1024]{0:T(1024)}, u32[]{:S(2)}) copy-start(s32[1024]{0:T(1024)} %constant.314) | copy-start | bytes 12292
  59.1 19.8 %all-to-all-start.2 = ((bf16[4,16,4096]{2,1,0:T(8,128)(2,1)}), bf16[4,16,4096]{2,1,0:T(8,128)(2,1)S(1)}, u32[]{:S(2)}, u32[]{:S(2)}) async-start(bf16[4,16,4096]{2,1,0:T(8,128)(2,1)} %bitcast.93), calls=%async_computation.2 | async-start | bytes 1048576 | tf_op jit(solution)/shard_map/all_to_all | solution.py:161
  64.2 604.2 %all-reduce.3.cloned.1.call-start = ((), (), s32[]{:S(2)}) async-start(), calls=%async_computation.5 | async-start | bytes 1048576
  81.0 569.8 %copy-start.12 = (u32[32]{0:T(128)S(1)}, u32[32]{0:T(128)}, u32[]{:S(2)}) copy-start(u32[32]{0:T(128)} %constant.249) | copy-start | bytes 388
  206.4 0.7 copy-start.1
  348.3 0.7 copy-start.1
  490.2 0.7 copy-start.1
  632.1 0.7 copy-start.1
  650.8 41.4 %reduce-scatter.5.cloned.1.call-start = ((), (), s32[]{:S(2)}) async-start(), calls=%async_computation.4 | async-start | bytes 327680 | tf_op jit(solution)/shard_map/reduce_scatter | solution.py:194
Sparse Core Ops, SparseCore 0:
  650.9 17.4 all-reduce.2
  671.3 20.8 reduce-scatter.4
where the time goes:
time: 709 us; the launch traced here: 699 us
  local copies, waits for them, and re-layouts  333 us (47%)
  other arithmetic  222 us (31%)
  waiting for transfers between devices  51 us (7%)
  matrix products  39.9 us (6%)
  starting transfers between devices  16.7 us (2%)
  between operations  14.2 us (2%)
  loops' own time  12.1 us (2%)
  blocking collectives  10.3 us (1%)
    dynamic_update_slice x128, other arithmetic, harmonic_table(): lax.scan(legendre_step, (zero_rows, zero_rows), (jnp.arange(degrees), jnp...  109 us
    mul x128, local copies, waits for them, and re-layouts, legendre_step(): coef_first[:, None]  90.6 us
    dynamic_slice x128, local copies, waits for them, and re-layouts, harmonic_table(): lax.scan(legendre_step, (zero_rows, zero_rows), (jnp.arange(degrees), jnp...  75.7 us
    eq x128, other arithmetic, legendre_step(): current = jnp.where((azimuths == degree)[:, None], diag_col, current)  72.2 us
    dynamic_update_slice x256, local copies, waits for them, and re-layouts, harmonic_table(): lax.scan(trig_step, (jnp.ones_like(along_x), jnp.zeros_like(along_x)), No...  52.4 us
    gather x4, local copies, waits for them, and re-layouts, harmonic_table(): jnp.take(legendre, jnp.asarray(pick_rows, jnp.int32), axis=0)  49.5 us
    dot_general x4, matrix products, add_angles(): lax.dot_general(harmonics, angle_plane, (((1,), (1,)), ((), ())), preferr...  31.7 us
    while x268, other arithmetic  30.7 us
  transfers between devices with their start and end apart: 5, of which 3 were waited for; matrix products, arithmetic and copies ran while one was open for 3% of the time, Pallas kernels for 0%

commit v1 on v0

v1 whole, which is shorter than its diff:
```python
import functools
import math

import jax
import jax.numpy as jnp
import numpy as np
from jax import lax
from jax.experimental import pallas as pl
from jax.experimental.pallas import tpu as pltpu
from jax.sharding import PartitionSpec as P

ANGLES = 64
ORDER = 32
BLOCK = 128
CPO = 8
COEF = 1024
HALF = 16
ROWS = 2 * HALF * HALF + 2 * (ORDER - HALF) * ORDER
LANES = 128
CHUNK = 256
MESH = pl.DeviceIdType.MESH


def legendre_constants(degrees):
    table = np.zeros((degrees, 2 * degrees), np.float32)
    diagonal = []
    running = 1.0
    for degree in range(degrees):
        for azimuth in range(degree):
            table[azimuth, degree] = math.sqrt(
                (4.0 * degree * degree - 1.0) / (degree * degree - azimuth * azimuth)
            )
            lower_term = max((degree - 1.0) ** 2 - azimuth * azimuth, 0.0)
            lower_den = max(4.0 * (degree - 1.0) ** 2 - 1.0, 1.0)
            table[azimuth, degrees + degree] = math.sqrt(lower_term / lower_den)
        if degree > 0:
            running = running * (2.0 * degree - 1.0) / (2.0 * degree)
        diagonal.append(math.sqrt((2.0 * degree + 1.0) / (4.0 * math.pi) * running))
    return table, diagonal


def padded_rows(degree):
    rows = HALF if degree < HALF else ORDER
    base = 2 * HALF * min(degree, HALF) + 2 * ORDER * max(degree - HALF, 0)
    return rows, base


def nt_dot(left, right):
    return lax.dot_general(
        left, right, (((1,), (1,)), ((), ())), preferred_element_type=jnp.float32
    )


def kernel(
    sizes,
    diagonal,
    images,
    references,
    weight,
    weight_col,
    weight_row,
    requests,
    slot_block,
    euler,
    order,
    lane_ids,
    constants,
    coef_out,
    evidence_out,
    image_buf,
    ref_buf,
    native,
    by_angle,
    wanted,
    eulers,
    picked,
    slices,
    shares,
    dir_rows,
    cos_rows,
    sin_rows,
    table,
    averages,
    padded,
    coef,
    ang_recv,
    rot_send,
    rot_recv,
    load_sem,
    req_sem,
    eul_sem,
    slice_sem,
    share_sem,
    ang_sem,
    rot_sem,
):
    owners, shell_size, ang_size, shells, angles, rots = sizes
    half = shells * angles
    cs = 2 * shells
    slots = owners * CPO
    dirs = slots * angles
    rows_out = COEF // (owners * ang_size)
    rot = lax.axis_index("rot")
    shell = lax.axis_index("shell")
    ang = lax.axis_index("ang")
    sharers = shell_size * ang_size
    lin = shell * ang_size + ang

    load_refs = pltpu.make_async_copy(references, ref_buf, load_sem.at[0])
    load_refs.start()
    columns = order.shape[1] // LANES
    load_images = []
    for h in range(columns):
        load_images.append(
            pltpu.make_async_copy(
                images.at[:, h * LANES : (h + 1) * LANES], image_buf.at[h], load_sem.at[1 + h]
            )
        )
        load_images[-1].start()

    rot_ids = [{"rot": lax.rem(rot + k, owners)} for k in range(1, owners)]
    share_ids = []
    for k in range(1, sharers):
        other = lax.rem(lin + k, sharers)
        share_ids.append({"shell": other // ang_size, "ang": lax.rem(other, ang_size)})
    barrier = pltpu.get_barrier_semaphore()
    for device in rot_ids + share_ids:
        pl.semaphore_signal(barrier, inc=1, device_id=device, device_id_type=MESH)
    pl.semaphore_wait(barrier, len(rot_ids) + len(share_ids))

    def send(src, dst, sems, device):
        copy = pltpu.make_async_remote_copy(
            src_ref=src,
            dst_ref=dst,
            send_sem=sems[0],
            recv_sem=sems[1],
            device_id=device,
            device_id_type=MESH,
        )
        copy.start()
        return copy

    sent = []
    small = []
    for k, device in enumerate(rot_ids):
        small.append(
            send(requests.at[device["rot"]], wanted.at[rot],
                 (req_sem.at[0, k], req_sem.at[1, k]), device)
        )
        small.append(send(euler, eulers.at[rot], (eul_sem.at[0, k], eul_sem.at[1, k]), device))
    wanted[rot] = requests[rot]
    eulers[rot] = euler[...]
    for copy in small:
        copy.wait_recv()
    sent += small

    load_refs.wait()
    ids = wanted[...].reshape(slots, LANES)[:, :1]
    selector = (ids == lax.broadcasted_iota(jnp.int32, (slots, rots), 1)).astype(jnp.float32)
    selector = selector.astype(jnp.bfloat16)
    for part in range(2):
        step = min(half, 1024)
        for start in range(0, half, step):
            found = nt_dot(selector, ref_buf[part * half + start : part * half + start + step, :])
            for owner in range(owners):
                picked[owner, part, :, start : start + step] = found[
                    owner * CPO : (owner + 1) * CPO
                ]
    for owner in range(owners):
        slices[owner] = picked[owner].reshape(2 * CPO, half).astype(jnp.bfloat16)
    moving = []
    for k, device in enumerate(rot_ids):
        moving.append(
            send(
                slices.at[device["rot"]],
                slices.at[owners + rot],
                (slice_sem.at[0, k], slice_sem.at[1, k]),
                device,
            )
        )
    slices[owners + rot] = slices[rot]

    for copy in load_images:
        copy.wait()

    @pl.loop(0, shells)
    def _(s):
        scale = weight[s]
        for part in range(2):
            at = pl.ds(pl.multiple_of(part * half + s * angles, angles), angles)
            for h in range(columns):
                native[at, h * LANES : (h + 1) * LANES] = (image_buf[h, at, :] * scale).astype(
                    jnp.bfloat16
                )

    for a in range(angles):
        for h in range(columns):
            by_angle[a * cs : (a + 1) * cs, h * LANES : (h + 1) * LANES] = (
                image_buf[h, pl.ds(a, cs, stride=angles), :] * weight_col[...]
            ).astype(jnp.bfloat16)

    dev_images = order.shape[1]
    member = order[...] == lax.broadcasted_iota(jnp.int32, (dev_images, dev_images), 0)
    member = member.astype(jnp.float32).astype(jnp.bfloat16)
    blocks = dev_images // BLOCK
    place = lax.broadcasted_iota(jnp.int32, (8, dev_images), 1)
    block_of = jnp.zeros((8, dev_images), jnp.float32)
    for b in range(1, blocks):
        block_of = jnp.where(place >= b * BLOCK, float(b), block_of)
    image_block = nt_dot(block_of.astype(jnp.bfloat16), member)[:1]

    lane_slot = lane_ids[0:1, :]
    angle = lane_ids[1:2, :] + (ang * angles).astype(jnp.float32)
    rows3 = [jnp.zeros((1, dirs), jnp.float32) for _ in range(3)]
    row_slot = lax.broadcasted_iota(jnp.int32, (CPO, dirs), 0).astype(jnp.float32)
    for owner in range(owners):
        hit = requests[owner][:, :1] == lax.broadcasted_iota(jnp.int32, (CPO, rots), 1)
        here = lane_slot == row_slot + float(owner * CPO)
        for i in range(3):
            value = jnp.sum(
                jnp.where(hit, eulers[owner][i : i + 1, :], 0.0), axis=1, keepdims=True
            )
            rows3[i] += jnp.sum(jnp.where(here, value, 0.0), axis=0, keepdims=True)
    phase = (2.0 * math.pi / ANGLES) * angle + rows3[2]
    cos_p, sin_p = jnp.cos(phase), jnp.sin(phase)
    cos_a, sin_a = jnp.cos(rows3[0]), jnp.sin(rows3[0])
    cos_b, sin_b = jnp.cos(rows3[1]), jnp.sin(rows3[1])
    x = cos_a * cos_b * cos_p - sin_a * sin_p
    y = sin_a * cos_b * cos_p + cos_a * sin_p
    dir_rows[...] = -sin_b * cos_p
    real = jnp.ones_like(x)
    imag = jnp.zeros_like(x)
    for m in range(ORDER):
        factor = math.sqrt(2.0) if m else 1.0
        cos_rows[m : m + 1, :] = real * factor
        sin_rows[m : m + 1, :] = imag * factor
        real, imag = x * real - y * imag, x * imag + y * real

    width = min(CHUNK, dirs)

    @pl.loop(0, dirs // width)
    def _(step):
        lanes = pl.ds(pl.multiple_of(step * width, width), width)
        z = dir_rows[:, lanes]
        prev = jnp.zeros((HALF, width), jnp.float32)
        early = prev
        for degree in range(ORDER):
            rows, base = padded_rows(degree)
            if degree == HALF:
                pad = jnp.zeros((ORDER - HALF, width), jnp.float32)
                prev = jnp.concatenate([prev, pad], axis=0)
                early = jnp.concatenate([early, pad], axis=0)
            first = constants[:rows, degree : degree + 1]
            second = constants[:rows, ORDER + degree : ORDER + degree + 1]
            now = first * (z * prev - second * early)
            azimuth = lax.broadcasted_iota(jnp.int32, (rows, width), 0)
            now = jnp.where(azimuth == degree, diagonal[degree], now)
            table[base : base + rows, lanes] = (now * cos_rows[:rows, lanes]).astype(jnp.bfloat16)
            table[base + rows : base + 2 * rows, lanes] = (now * sin_rows[:rows, lanes]).astype(
                jnp.bfloat16
            )
            prev, early = now, prev

    for copy in moving:
        copy.wait_recv()
    sent += moving
    got = slices[owners:].reshape(owners * 2 * CPO, half)
    squares = jnp.square(got.astype(jnp.float32)) * weight_row[...]
    norms = jnp.sum(squares, axis=1, keepdims=True)
    low = jnp.dot(got, native[:half, :], preferred_element_type=jnp.float32)
    high = jnp.dot(got, native[half:, :], preferred_element_type=jnp.float32)
    low = (2.0 * low - norms).reshape(owners, 2, CPO, dev_images)[:, 0]
    high = (2.0 * high - norms).reshape(owners, 2, CPO, dev_images)[:, 1]
    shares[lin] = (low + high).reshape(slots, dev_images)
    moving = []
    for k, device in enumerate(share_ids):
        moving.append(
            send(shares.at[lin], shares.at[lin], (share_sem.at[0, k], share_sem.at[1, k]), device)
        )
    for copy in moving:
        copy.wait_recv()
    sent += moving
    scores = shares[0]
    for k in range(1, sharers):
        scores = scores + shares[k]

    valid = slot_block[:, :1] == image_block
    masked = jnp.where(valid, scores, -3.0e38)
    highest = jnp.max(masked, axis=0, keepdims=True)
    total = jnp.sum(jnp.where(valid, jnp.exp(masked - highest), 0.0), axis=0, keepdims=True)
    evidence = highest + jnp.log(total)
    evidence_out[...] = evidence
    weights = jnp.where(valid, jnp.exp(masked - evidence), 0.0).astype(jnp.bfloat16)

    if cs < averages.shape[1]:
        averages[...] = jnp.zeros(averages.shape, jnp.bfloat16)
    for a in range(angles):
        averages[a * slots : (a + 1) * slots, :cs] = nt_dot(
            weights, by_angle[a * cs : (a + 1) * cs, :]
        ).astype(jnp.bfloat16)

    tile = 256

    @pl.loop(0, ROWS // tile)
    def _(step):
        at = pl.ds(pl.multiple_of(step * tile, tile), tile)
        padded[at, :] = jnp.dot(table[at, :], averages[...], preferred_element_type=jnp.float32)

    for degree in range(ORDER):
        rows, base = padded_rows(degree)
        first = degree * degree
        coef[first : first + 1, :] = padded[base : base + 1, :]
        if degree:
            coef[pl.ds(first + 1, degree, stride=2), :] = padded[base + 1 : base + 1 + degree, :]
            coef[pl.ds(first + 2, degree, stride=2), :] = padded[
                base + rows + 1 : base + rows + 1 + degree, :
            ]

    def out_rows(rot_id, ang_id):
        return pl.ds(pl.multiple_of((rot_id * ang_size + ang_id) * rows_out, rows_out), rows_out)

    turns = [lax.rem(rot + j, owners) for j in range(1, owners + 1)]
    across = []
    for j, rot_id in enumerate(turns):
        line = []
        for k in range(1, ang_size):
            other = lax.rem(ang + k, ang_size)
            line.append(
                send(
                    coef.at[out_rows(rot_id, other)],
                    ang_recv.at[k - 1, j],
                    (ang_sem.at[0, k - 1, j], ang_sem.at[1, k - 1, j]),
                    {"ang": other},
                )
            )
        across.append(line)
    moving = []
    for j, rot_id in enumerate(turns):
        total_here = coef[out_rows(rot_id, ang), :]
        for k, copy in enumerate(across[j]):
            copy.wait_recv()
            total_here = total_here + ang_recv[k, j]
        sent += across[j]
        if j < owners - 1:
            rot_send[j] = total_here.astype(jnp.bfloat16)
            moving.append(
                send(
                    rot_send.at[j],
                    rot_recv.at[j],
                    (rot_sem.at[0, j], rot_sem.at[1, j]),
                    {"rot": rot_id},
                )
            )
    for j, copy in enumerate(moving):
        copy.wait_recv()
        total_here = total_here + rot_recv[j].astype(jnp.float32)
    sent += moving
    coef_out[...] = total_here
    for copy in sent:
        copy.wait_send()


def per_device(
    images, references, noise_weight, euler_angles, candidate_count, candidate_rotation, image_order
):
    owners = lax.axis_size("rot")
    shell_size = lax.axis_size("shell")
    ang_size = lax.axis_size("ang")
    _, shells, angles, dev_images = images.shape
    rots = references.shape[3]
    features = 2 * shells * angles
    half = shells * angles
    cs = 2 * shells
    slots = owners * CPO
    dirs = slots * angles
    sharers = shell_size * ang_size
    rows_out = COEF // (owners * ang_size)
    wide = max(cs, LANES)

    place = jnp.arange(CPO)[None, :]
    offset = jnp.zeros((owners, 1), jnp.int32)
    rotation = jnp.zeros((owners, CPO), jnp.int32)
    slot_block = jnp.full((owners, CPO), -1.0, jnp.float32)
    for b in range(candidate_count.shape[0]):
        count = candidate_count[b][:, None]
        local = place - offset
        inside = (local >= 0) & (local < count)
        match = inside[:, :, None] & (local[:, :, None] == jnp.arange(CPO))
        rotation += jnp.sum(jnp.where(match, candidate_rotation[b][:, None, :], 0), axis=2)
        slot_block = jnp.where(inside, float(b), slot_block)
        offset = offset + count
    requests = jnp.broadcast_to(rotation[:, :, None], (owners, CPO, LANES))
    slot_block = jnp.broadcast_to(slot_block.reshape(slots, 1), (slots, LANES))

    table, diagonal = legendre_constants(ORDER)
    lane = np.arange(dirs)
    lane_ids = np.stack([lane % slots, lane // slots]).astype(np.float32)
    vmem = pl.BlockSpec(memory_space=pltpu.VMEM)
    hbm = pl.BlockSpec(memory_space=pl.ANY)
    smem = pl.BlockSpec(memory_space=pltpu.SMEM)
    sizes = (owners, shell_size, ang_size, shells, angles, rots)
    f32, bf16 = jnp.float32, jnp.bfloat16
    dma = pltpu.SemaphoreType.DMA
    coefficients, evidence = pl.pallas_call(
        functools.partial(kernel, sizes, diagonal),
        out_shape=(
            jax.ShapeDtypeStruct((rows_out, wide), f32),
            jax.ShapeDtypeStruct((1, dev_images), f32),
        ),
        in_specs=[hbm, hbm, smem] + [vmem] * 8,
        out_specs=(vmem, vmem),
        scratch_shapes=[
            pltpu.VMEM((dev_images // LANES, features, LANES), f32),
            pltpu.VMEM((features, rots), bf16),
            pltpu.VMEM((features, dev_images), bf16),
            pltpu.VMEM((features, dev_images), bf16),
            pltpu.VMEM((owners, CPO, LANES), jnp.int32),
            pltpu.VMEM((owners, 3, rots), f32),
            pltpu.VMEM((owners, 2, CPO, half), f32),
            pltpu.VMEM((2 * owners, 2 * CPO, half), bf16),
            pltpu.VMEM((sharers, slots, dev_images), f32),
            pltpu.VMEM((1, dirs), f32),
            pltpu.VMEM((ORDER, dirs), f32),
            pltpu.VMEM((ORDER, dirs), f32),
            pltpu.VMEM((ROWS, dirs), bf16),
            pltpu.VMEM((dirs, wide), bf16),
            pltpu.VMEM((ROWS, wide), f32),
            pltpu.VMEM((COEF, wide), f32),
            pltpu.VMEM((max(ang_size - 1, 1), owners, rows_out, wide), f32),
            pltpu.VMEM((max(owners - 1, 1), rows_out, wide), bf16),
            pltpu.VMEM((max(owners - 1, 1), rows_out, wide), bf16),
            dma((1 + dev_images // LANES,)),
            dma((2, max(owners - 1, 1))),
            dma((2, max(owners - 1, 1))),
            dma((2, max(owners - 1, 1))),
            dma((2, max(sharers - 1, 1))),
            dma((2, max(ang_size - 1, 1), owners)),
            dma((2, max(owners - 1, 1))),
        ],
        compiler_params=pltpu.CompilerParams(
            collective_id=0, has_side_effects=True, vmem_limit_bytes=60 * 1024 * 1024
        ),
    )(
        images.reshape(features, dev_images),
        references.reshape(features, rots),
        noise_weight,
        jnp.concatenate([noise_weight, noise_weight])[:, None],
        jnp.repeat(noise_weight, angles)[None, :],
        requests,
        slot_block,
        euler_angles,
        image_order[None, :],
        jnp.asarray(lane_ids),
        jnp.asarray(table),
    )
    return (coefficients[:, :cs].reshape(rows_out, 2, shells), evidence.reshape(dev_images))


def solution(mesh):
    in_specs = (
        P(None, "shell", "ang", ("grp", "rot")),
        P(None, "shell", "ang", ("grp", "rot")),
        P(("grp", "shell")),
        P(None, ("grp", "rot")),
        P(("grp", "rot"), None),
        P(("grp", "rot"), None, None),
        P(("grp", "rot")),
    )
    out_specs = (P(("grp", "rot", "ang"), None, "shell"), P(("grp", "rot")))
    return jax.shard_map(
        per_device, mesh=mesh, in_specs=in_specs, out_specs=out_specs, check_vma=False
    )
```

time: 709 us -> 40.3 us (0.06); the launches traced: 699 us -> 40 us
  local copies, waits for them, and re-layouts: 333 us -> 7.84 us
  other arithmetic: 222 us -> 1.33 us
  waiting for transfers between devices: 51 us -> 0 us
  matrix products: 39.9 us -> 0 us
  Pallas kernels: 0 us -> 30.1 us
  starting transfers between devices: 16.7 us -> 0 us
  between operations: 14.2 us -> 0.65 us
  loops' own time: 12.1 us -> 0 us
  blocking collectives: 10.3 us -> 0 us
    dynamic_update_slice x128 -> x0, other arithmetic: 109 us -> none  [harmonic_table(): lax.scan(legendre_step, (zero_rows, zero_rows), (jnp.arange(degrees), jnp...]
    mul x129 -> x0, local copies, waits for them, and re-layouts: 90.7 us -> none  [the longest x128 90.6 us: legendre_step(): coef_first[:, None]]
    gather x10 -> x0, local copies, waits for them, and re-layouts: 88.2 us -> none  [the longest x4 49.5 us: harmonic_table(): jnp.take(legendre, jnp.asarray(pick_rows, jnp.int32), axis=0)]
    dynamic_slice x132 -> x0, local copies, waits for them, and re-layouts: 80 us -> none  [the longest x128 75.7 us: harmonic_table(): lax.scan(legendre_step, (zero_rows, zero_rows), (jnp.arange(degrees), jnp...]
    eq x128 -> x0, other arithmetic: 72.2 us -> none  [legendre_step(): current = jnp.where((azimuths == degree)[:, None], diag_col, current)]
    dynamic_update_slice x256 -> x0, local copies, waits for them, and re-layouts: 52.4 us -> none  [harmonic_table(): lax.scan(trig_step, (jnp.ones_like(along_x), jnp.zeros_like(along_x)), No...]
    dot_general x7 -> x0, matrix products: 37.4 us -> none  [the longest x4 31.7 us: add_angles(): lax.dot_general(harmonics, angle_plane, (((1,), (1,)), ((), ())), preferr...]
    while x268 -> x0, other arithmetic: 30.7 us -> none
  transfers between devices with their start and end apart: 5 -> 0, of which waited for: 3 -> 0; matrix products, arithmetic and copies ran while one was open for 3% -> 0% of each run, Pallas kernels for 0% -> 0%
where the time goes in v1:
time: 40.3 us; the launch traced here: 40 us
  Pallas kernels  30.1 us (75%)
  local copies, waits for them, and re-layouts  7.84 us (19%)
  other arithmetic  1.33 us (3%)
  between operations  0.65 us (2%)
    pallas_call x1, Pallas kernels, per_device(): pl.pallas_call(functools.partial(kernel, sizes, diagonal), out_shape=(jax...  30.1 us
    pallas_call x1, local copies, waits for them, and re-layouts, per_device(): pl.pallas_call(functools.partial(kernel, sizes, diagonal), out_shape=(jax...  1.57 us
    unnamed x1, local copies, waits for them, and re-layouts  1.24 us
    broadcast_in_dim x1, other arithmetic, per_device(): jnp.concatenate([noise_weight, noise_weight])[:, None]  0.81 us

profile of v1, /device:TPU:0, one launch (start us, length us, event | category | flops | bytes accessed | tf_op | source)
XLA Modules:
  0.0 40.0 jit_solution(11869303873331117230)
XLA Ops:
  0.6 0.8 %maximum_bitcast_fusion = f32[128,1]{0,1:T(1,128)S(1)} fusion(f32[64]{0:T(128)} %weight.1), kind=kLoop, calls=%fused_computation.12 | loop fusion | flops 128 | bytes 768 | tf_op jit(solution)/shard_map/broadcast_in_dim | solution.py:447
  1.4 0.8 %slice_bitcast_fusion.2 = (s32[4]{0:T(128)S(1)}, s32[4]{0:T(128)S(1)}) fusion(s32[2,4]{1,0:T(2,128)} %param.13), kind=kLoop, calls=%fused_computation.13 | loop fusion | bytes 64 | tf_op jit(solution)/shard_map/lt | solution.py:387
  2.2 0.1 iota_compare_fusion.2
  2.3 0.1 iota_subtract_fusion
  2.3 0.1 select_select_fusion
  2.4 0.1 select_n.30
  2.5 0.7 %slice_bitcast_fusion = (s32[4,8]{1,0:T(4,128)S(1)}, s32[4,8]{1,0:T(4,128)S(1)}) fusion(s32[2,4,8]{2,1,0:T(4,128)} %param.14), kind=kLoop, calls=%fused_computation.7 | loop fusion | bytes 512 | tf_op jit(solution)/shard_map/jit(_where)/broadcast_in_dim | solution.py:389
  3.2 0.3 select_reduce_fusion
  3.5 0.7 %broadcast_in_dim.66.requests = s32[4,8,128]{2,1,0:T(8,128)} broadcast(s32[4,8]{1,0:T(4,128)S(1)} %add.7), dimensions={0,1} | broadcast | bytes 16512 | tf_op jit(solution)/shard_map/broadcast_in_dim | solution.py:392
  4.2 0.7 %broadcast_in_dim.70.slot_block = f32[32,128]{1,0:T(8,128)} broadcast(f32[32]{0:T(128)S(1)} %select_n.30), dimensions={0} | broadcast | bytes 16512 | tf_op jit(solution)/shard_map/broadcast_in_dim | solution.py:393
  4.8 0.7 %broadcast_in_dim.60 = f32[64,32]{1,0:T(8,128)S(1)} broadcast(f32[64]{0:T(128)} %weight.1), dimensions={0} | broadcast | bytes 8448 | tf_op jit(solution)/shard_map/broadcast_in_dim | solution.py:448
  5.6 0.7 %broadcast_in_dim_reshape.3.weight_row = f32[1,2048]{1,0:T(1,128)} reshape(f32[64,32]{1,0:T(8,128)S(1)} %broadcast_in_dim.60) | data formatting | bytes 16384 | tf_op jit(solution)/shard_map/broadcast_in_dim;reshape | solution.py:448
  6.3 0.7 %copy.15.weight_col = f32[128,1]{1,0:T(8,128)} copy(f32[128,1]{0,1:T(1,128)S(1)} %maximum_bitcast_fusion) | data formatting | bytes 1024 | tf_op jit(solution)/shard_map/broadcast_in_dim | solution.py:447
  7.0 30.1 %shard_map.104 = (f32[128,128]{1,0:T(8,128)}, f32[1,256]{1,0:T(1,128)}) custom-call(f32[4096,256]{1,0:T(8,128)} %bitcast.15, bf16[4096,256]{1,0:T(8,128)(2,1)} %bitcast.16, f32[64]{0:T(128)} %weight.1, f32[128,1]{1,0:T(8,128)} %copy.15.weight_col, f32[1,2048]{1,0:T(1,128)} %broadcast_in_dim_reshape.3.weight_row, s32[4,8,128]{2,1,0:T(8,128)} %broadcast_in_dim.66.requests, ...), custom_call_target="tpu_custom_call" | custom-call | tf_op jit(solution)/shard_map/pallas_call | solution.py:404
  37.2 1.6 %copy.16 = f32[128,128]{0,1:T(8,128)} copy(f32[128,128]{1,0:T(8,128)} %get-tuple-element.4) | data formatting | bytes 131072 | tf_op jit(solution)/shard_map/pallas_call | solution.py:404
  38.7 1.2 %copy.18 = f32[256]{0:T(256)} copy(f32[256]{0:T(256)} %bitcast.19) | data formatting | bytes 2048
  (1 shorter events, 0.0 us)

commit v2 on v1

v2 whole, which is shorter than its diff:
```python
import functools
import math

import jax
import jax.numpy as jnp
import numpy as np
from jax import lax
from jax.experimental import pallas as pl
from jax.experimental.pallas import tpu as pltpu
from jax.sharding import PartitionSpec as P

ANGLES = 64
ORDER = 32
BLOCK = 128
CPO = 8
COEF = 1024
HALF = 16
ROWS = 2 * HALF * HALF + 2 * (ORDER - HALF) * ORDER
LANES = 128
CHUNK = 256
MESH = pl.DeviceIdType.MESH


def legendre_constants(degrees):
    table = np.zeros((degrees, 2 * degrees), np.float32)
    diagonal = []
    running = 1.0
    for degree in range(degrees):
        for azimuth in range(degree):
            table[azimuth, degree] = math.sqrt(
                (4.0 * degree * degree - 1.0) / (degree * degree - azimuth * azimuth)
            )
            lower_term = max((degree - 1.0) ** 2 - azimuth * azimuth, 0.0)
            lower_den = max(4.0 * (degree - 1.0) ** 2 - 1.0, 1.0)
            table[azimuth, degrees + degree] = math.sqrt(lower_term / lower_den)
        if degree > 0:
            running = running * (2.0 * degree - 1.0) / (2.0 * degree)
        diagonal.append(math.sqrt((2.0 * degree + 1.0) / (4.0 * math.pi) * running))
    return table, diagonal


def padded_rows(degree):
    rows = HALF if degree < HALF else ORDER
    base = 2 * HALF * min(degree, HALF) + 2 * ORDER * max(degree - HALF, 0)
    return rows, base


def nt_dot(left, right):
    return lax.dot_general(
        left, right, (((1,), (1,)), ((), ())), preferred_element_type=jnp.float32
    )


def kernel(
    sizes,
    diagonal,
    images,
    references,
    weight_in,
    count_in,
    rotation_in,
    euler_in,
    order_in,
    constants_in,
    out,
    image_buf,
    ref_buf,
    native,
    by_angle,
    weight_row,
    counts,
    rotations,
    euler,
    order,
    constants,
    weight_tile,
    requests,
    slot_block,
    wanted,
    eulers,
    slices,
    shares,
    dir_rows,
    cos_rows,
    sin_rows,
    table,
    averages,
    padded,
    coef,
    ang_recv,
    rot_own,
    rot_send,
    rot_recv,
    load_sem,
    req_sem,
    eul_sem,
    slice_sem,
    share_sem,
    ang_sem,
    rot_sem,
):
    owners, shell_size, ang_size, shells, angles, rots = sizes
    half = shells * angles
    cs = 2 * shells
    slots = owners * CPO
    dirs = slots * angles
    rows_out = COEF // (owners * ang_size)
    dev_images = order.shape[1]
    columns = dev_images // LANES
    blocks = counts.shape[0]
    rot = lax.axis_index("rot")
    shell = lax.axis_index("shell")
    ang = lax.axis_index("ang")
    sharers = shell_size * ang_size
    lin = shell * ang_size + ang

    loads = []

    def load(src, dst):
        copy = pltpu.make_async_copy(src, dst, load_sem.at[len(loads)])
        copy.start()
        loads.append(copy)

    load(count_in, counts)
    load(rotation_in, rotations)
    load(euler_in, euler)
    load(weight_in, weight_row)
    load(order_in, order)
    load(constants_in, constants)
    load(references, ref_buf)
    for h in range(columns):
        load(images.at[:, h * LANES : (h + 1) * LANES], image_buf.at[h])

    rot_ids = [{"rot": lax.rem(rot + k, owners)} for k in range(1, owners)]
    share_ids = []
    for k in range(1, sharers):
        other = lax.rem(lin + k, sharers)
        share_ids.append({"shell": other // ang_size, "ang": lax.rem(other, ang_size)})
    barrier = pltpu.get_barrier_semaphore()
    for device in rot_ids + share_ids:
        pl.semaphore_signal(barrier, inc=1, device_id=device, device_id_type=MESH)

    def send(src, dst, sems, device):
        copy = pltpu.make_async_remote_copy(
            src_ref=src,
            dst_ref=dst,
            send_sem=sems[0],
            recv_sem=sems[1],
            device_id=device,
            device_id_type=MESH,
        )
        copy.start()
        return copy

    for copy in loads[:3]:
        copy.wait()
    place = lax.broadcasted_iota(jnp.int32, (CPO, CPO), 0).astype(jnp.float32)
    entry = lax.broadcasted_iota(jnp.int32, (CPO, CPO), 1).astype(jnp.float32)
    for owner in range(owners):
        local = place
        rotation = jnp.zeros((CPO, 1), jnp.float32)
        block = jnp.full((CPO, CPO), -1.0, jnp.float32)
        for b in range(blocks):
            count = counts[b : b + 1, owner : owner + 1].astype(jnp.float32)
            listed = rotations[b][owner : owner + 1, :].astype(jnp.float32)
            inside = (local >= 0.0) & (local < count)
            rotation += jnp.sum(
                jnp.where(inside & (local == entry), listed, 0.0), axis=1, keepdims=True
            )
            block = jnp.where(inside, float(b), block)
            local = local - count
        requests[owner] = jnp.broadcast_to(rotation, (CPO, LANES)).astype(jnp.int32)
        slot_block[owner * CPO : (owner + 1) * CPO, :] = jnp.broadcast_to(
            block[:, :1], (CPO, LANES)
        )
    wanted[rot] = requests[rot]
    eulers[rot] = euler[...]

    pl.semaphore_wait(barrier, len(rot_ids) + len(share_ids))
    sent = []
    small = []
    for k, device in enumerate(rot_ids):
        small.append(
            send(requests.at[device["rot"]], wanted.at[rot],
                 (req_sem.at[0, k], req_sem.at[1, k]), device)
        )
    late = []
    for k, device in enumerate(rot_ids):
        late.append(send(euler, eulers.at[rot], (eul_sem.at[0, k], eul_sem.at[1, k]), device))

    loads[3].wait()
    diag = lax.broadcasted_iota(jnp.int32, (shells, shells), 0) == lax.broadcasted_iota(
        jnp.int32, (shells, shells), 1
    )
    weight_col = jnp.sum(jnp.where(diag, weight_row[...], 0.0), axis=1, keepdims=True)
    weight_tile[...] = jnp.broadcast_to(weight_col, (shells, LANES))
    shell_at = lax.broadcasted_iota(jnp.int32, (shells, half), 0) * angles
    lane_at = lax.broadcasted_iota(jnp.int32, (shells, half), 1)
    spread = (lane_at >= shell_at) & (lane_at < shell_at + angles)
    weight_lanes = jnp.sum(jnp.where(spread, weight_col, 0.0), axis=0, keepdims=True)

    for copy in loads[7:]:
        copy.wait()

    def weigh(s, carry):
        scale = weight_tile[pl.ds(s, 1), :]
        for part in range(2):
            at = pl.ds(pl.multiple_of(part * half + s * angles, angles), angles)
            for h in range(columns):
                native[at, h * LANES : (h + 1) * LANES] = (image_buf[h, at, :] * scale).astype(
                    jnp.bfloat16
                )
        return carry

    lax.fori_loop(0, shells, weigh, 0, unroll=4)

    for copy in small:
        copy.wait_recv()
    sent += small
    loads[6].wait()
    ids = wanted[...].reshape(slots, LANES)[:, :1]
    selector = (ids == lax.broadcasted_iota(jnp.int32, (slots, rots), 1)).astype(jnp.float32)
    selector = selector.astype(jnp.bfloat16)
    step = min(half, 1024)
    pieces = half // step
    moving = []
    for piece in range(pieces):
        start = piece * step
        low = nt_dot(selector, ref_buf[start : start + step, :])
        high = nt_dot(selector, ref_buf[half + start : half + start + step, :])
        for owner in range(owners):
            at = slice(owner * CPO, (owner + 1) * CPO)
            slices[owner, :, start : start + step] = jnp.concatenate(
                [low[at], high[at]], axis=0
            ).astype(jnp.bfloat16)
        line = []
        for k, device in enumerate(rot_ids):
            line.append(
                send(
                    slices.at[device["rot"], :, start : start + step],
                    slices.at[owners + rot, :, start : start + step],
                    (slice_sem.at[0, piece, k], slice_sem.at[1, piece, k]),
                    device,
                )
            )
        moving.append(line)
    slices[owners + rot] = slices[rot]

    for a in range(angles):
        for part in range(2):
            for h in range(columns):
                by_angle[
                    a * cs + part * shells : a * cs + (part + 1) * shells,
                    h * LANES : (h + 1) * LANES,
                ] = (
                    image_buf[h, pl.ds(part * half + a, shells, stride=angles), :]
                    * weight_tile[...]
                ).astype(jnp.bfloat16)

    loads[4].wait()
    member = order[...] == lax.broadcasted_iota(jnp.int32, (dev_images, dev_images), 0)
    member = member.astype(jnp.float32).astype(jnp.bfloat16)
    position = lax.broadcasted_iota(jnp.int32, (8, dev_images), 1)
    block_of = jnp.zeros((8, dev_images), jnp.float32)
    for b in range(1, blocks):
        block_of = jnp.where(position >= b * BLOCK, float(b), block_of)
    image_block = nt_dot(block_of.astype(jnp.bfloat16), member)[:1]

    for copy in late:
        copy.wait_recv()
    sent += late
    lane = lax.broadcasted_iota(jnp.int32, (1, dirs), 1).astype(jnp.float32)
    angle = jnp.floor((lane + 0.5) * (1.0 / slots))
    lane_slot = lane - angle * slots
    angle = angle + (ang * angles).astype(jnp.float32)
    rows3 = [jnp.zeros((1, dirs), jnp.float32) for _ in range(3)]
    row_slot = lax.broadcasted_iota(jnp.int32, (CPO, dirs), 0).astype(jnp.float32)
    for owner in range(owners):
        hit = requests[owner][:, :1] == lax.broadcasted_iota(jnp.int32, (CPO, rots), 1)
        here = lane_slot == row_slot + float(owner * CPO)
        for i in range(3):
            value = jnp.sum(
                jnp.where(hit, eulers[owner][i : i + 1, :], 0.0), axis=1, keepdims=True
            )
            rows3[i] += jnp.sum(jnp.where(here, value, 0.0), axis=0, keepdims=True)
    phase = (2.0 * math.pi / ANGLES) * angle + rows3[2]
    cos_p, sin_p = jnp.cos(phase), jnp.sin(phase)
    cos_a, sin_a = jnp.cos(rows3[0]), jnp.sin(rows3[0])
    cos_b, sin_b = jnp.cos(rows3[1]), jnp.sin(rows3[1])
    x = cos_a * cos_b * cos_p - sin_a * sin_p
    y = sin_a * cos_b * cos_p + cos_a * sin_p
    dir_rows[...] = -sin_b * cos_p
    real = jnp.ones_like(x)
    imag = jnp.zeros_like(x)
    for m in range(ORDER):
        factor = math.sqrt(2.0) if m else 1.0
        cos_rows[m : m + 1, :] = real * factor
        sin_rows[m : m + 1, :] = imag * factor
        real, imag = x * real - y * imag, x * imag + y * real

    loads[5].wait()
    width = min(CHUNK, dirs)

    @pl.loop(0, dirs // width)
    def _(turn):
        lanes = pl.ds(pl.multiple_of(turn * width, width), width)
        z = dir_rows[:, lanes]
        prev = jnp.zeros((HALF, width), jnp.float32)
        early = prev
        for degree in range(ORDER):
            rows, base = padded_rows(degree)
            if degree == HALF:
                pad = jnp.zeros((ORDER - HALF, width), jnp.float32)
                prev = jnp.concatenate([prev, pad], axis=0)
                early = jnp.concatenate([early, pad], axis=0)
            first = constants[:rows, degree : degree + 1]
            second = constants[:rows, ORDER + degree : ORDER + degree + 1]
            now = first * (z * prev - second * early)
            azimuth = lax.broadcasted_iota(jnp.int32, (rows, width), 0)
            now = jnp.where(azimuth == degree, diagonal[degree], now)
            table[base : base + rows, lanes] = (now * cos_rows[:rows, lanes]).astype(jnp.bfloat16)
            table[base + rows : base + 2 * rows, lanes] = (now * sin_rows[:rows, lanes]).astype(
                jnp.bfloat16
            )
            prev, early = now, prev

    partial = jnp.zeros((slots, dev_images), jnp.float32)
    for piece in range(pieces):
        for copy in moving[piece]:
            copy.wait_recv()
        sent += moving[piece]
        start = piece * step
        got = slices[owners:, :, start : start + step].reshape(owners * 2 * CPO, step)
        squares = jnp.square(got.astype(jnp.float32)) * weight_lanes[:, start : start + step]
        norms = jnp.sum(squares, axis=1, keepdims=True)
        low = jnp.dot(got, native[start : start + step, :], preferred_element_type=jnp.float32)
        high = jnp.dot(
            got, native[half + start : half + start + step, :], preferred_element_type=jnp.float32
        )
        low = (2.0 * low - norms).reshape(owners, 2, CPO, dev_images)[:, 0]
        high = (2.0 * high - norms).reshape(owners, 2, CPO, dev_images)[:, 1]
        partial = partial + (low + high).reshape(slots, dev_images)
    shares[lin] = partial
    moving = []
    for k, device in enumerate(share_ids):
        moving.append(
            send(shares.at[lin], shares.at[lin], (share_sem.at[0, k], share_sem.at[1, k]), device)
        )
    for copy in moving:
        copy.wait_recv()
    sent += moving
    scores = shares[0]
    for k in range(1, sharers):
        scores = scores + shares[k]

    valid = slot_block[:, :1] == image_block
    masked = jnp.where(valid, scores, -3.0e38)
    highest = jnp.max(masked, axis=0, keepdims=True)
    total = jnp.sum(jnp.where(valid, jnp.exp(masked - highest), 0.0), axis=0, keepdims=True)
    evidence = highest + jnp.log(total)
    weights = jnp.where(valid, jnp.exp(masked - evidence), 0.0).astype(jnp.bfloat16)

    if cs < averages.shape[1]:
        averages[...] = jnp.zeros(averages.shape, jnp.bfloat16)
    for a in range(angles):
        averages[a * slots : (a + 1) * slots, :cs] = nt_dot(
            weights, by_angle[a * cs : (a + 1) * cs, :]
        ).astype(jnp.bfloat16)

    def out_rows(rot_id, ang_id):
        return pl.ds(pl.multiple_of((rot_id * ang_size + ang_id) * rows_out, rows_out), rows_out)

    across = []

    def start_across(j):
        line = []
        for k in range(1, ang_size):
            other = lax.rem(ang + k, ang_size)
            line.append(
                send(
                    coef.at[out_rows(j, other)],
                    ang_recv.at[k - 1, j],
                    (ang_sem.at[0, k - 1, j], ang_sem.at[1, k - 1, j]),
                    {"ang": other},
                )
            )
        across.append(line)

    def toward(j):
        return pltpu.make_async_remote_copy(
            src_ref=rot_send.at[j],
            dst_ref=rot_recv.at[rot],
            send_sem=rot_sem.at[0, j],
            recv_sem=rot_sem.at[1, rot],
            device_id={"rot": j},
            device_id_type=MESH,
        )

    def start_along(j):
        total_here = coef[out_rows(j, ang), :]
        for k, copy in enumerate(across[j]):
            copy.wait_recv()
            total_here = total_here + ang_recv[k, j]

        @pl.when(rot == j)
        def _():
            rot_own[...] = total_here

        @pl.when(rot != j)
        def _():
            rot_send[j] = total_here.astype(jnp.bfloat16)
            toward(j).start()

    tile = 256
    done = 0
    degree = 0
    for block in range(ROWS // tile):
        at = slice(block * tile, (block + 1) * tile)
        padded[at, :] = jnp.dot(table[at, :], averages[...], preferred_element_type=jnp.float32)
        while degree < ORDER and sum(padded_rows(degree)) + padded_rows(degree)[0] <= at.stop:
            rows, base = padded_rows(degree)
            first = degree * degree
            coef[first : first + 1, :] = padded[base : base + 1, :]
            if degree:
                coef[pl.ds(first + 1, degree, stride=2), :] = padded[base + 1 : base + 1 + degree]
                coef[pl.ds(first + 2, degree, stride=2), :] = padded[
                    base + rows + 1 : base + rows + 1 + degree
                ]
            degree += 1
        while done < owners and (done + 1) * ang_size * rows_out <= degree * degree:
            start_across(done)
            done += 1
            if done > 1:
                start_along(done - 2)
    start_along(owners - 1)

    total_here = rot_own[...]
    for k in range(1, owners):
        source = lax.rem(rot + k, owners)
        pltpu.make_async_remote_copy(
            src_ref=rot_send.at[0],
            dst_ref=rot_recv.at[source],
            send_sem=rot_sem.at[0, 0],
            recv_sem=rot_sem.at[1, source],
            device_id={"rot": source},
            device_id_type=MESH,
        ).wait_recv()
        total_here = total_here + rot_recv[source].astype(jnp.float32)
    out[0 : total_here.shape[1], 0:rows_out] = jnp.transpose(total_here)
    for h in range(columns):
        row = total_here.shape[1] + h
        out[row : row + 1, 0:LANES] = evidence[:, h * LANES : (h + 1) * LANES]
    for copy in sent:
        copy.wait_send()
    for line in across:
        for copy in line:
            copy.wait_send()
    for j in range(owners):

        @pl.when(rot != j)
        def _():
            toward(j).wait_send()


def per_device(
    images, references, noise_weight, euler_angles, candidate_count, candidate_rotation, image_order
):
    owners = lax.axis_size("rot")
    shell_size = lax.axis_size("shell")
    ang_size = lax.axis_size("ang")
    _, shells, angles, dev_images = images.shape
    rots = references.shape[3]
    features = 2 * shells * angles
    half = shells * angles
    cs = 2 * shells
    slots = owners * CPO
    dirs = slots * angles
    sharers = shell_size * ang_size
    rows_out = COEF // (owners * ang_size)
    wide = max(cs, LANES)

    table, diagonal = legendre_constants(ORDER)
    vmem = pl.BlockSpec(memory_space=pltpu.VMEM)
    hbm = pl.BlockSpec(memory_space=pl.ANY)
    sizes = (owners, shell_size, ang_size, shells, angles, rots)
    f32, bf16 = jnp.float32, jnp.bfloat16
    dma = pltpu.SemaphoreType.DMA
    out_lanes = max(rows_out, LANES)
    columns = dev_images // LANES
    blocks = candidate_count.shape[0]
    others = max(owners - 1, 1)
    pieces = half // min(half, 1024)
    result = pl.pallas_call(
        functools.partial(kernel, sizes, diagonal),
        out_shape=jax.ShapeDtypeStruct((wide + 8, out_lanes), f32),
        in_specs=[hbm] * 8,
        out_specs=vmem,
        scratch_shapes=[
            pltpu.VMEM((columns, features, LANES), f32),
            pltpu.VMEM((features, rots), bf16),
            pltpu.VMEM((features, dev_images), bf16),
            pltpu.VMEM((features, dev_images), bf16),
            pltpu.VMEM((1, shells), f32),
            pltpu.VMEM((blocks, owners), jnp.int32),
            pltpu.VMEM((blocks, owners, CPO), jnp.int32),
            pltpu.VMEM((3, rots), f32),
            pltpu.VMEM((1, dev_images), jnp.int32),
            pltpu.VMEM(table.shape, f32),
            pltpu.VMEM((shells, LANES), f32),
            pltpu.VMEM((owners, CPO, LANES), jnp.int32),
            pltpu.VMEM((slots, LANES), f32),
            pltpu.VMEM((owners, CPO, LANES), jnp.int32),
            pltpu.VMEM((owners, 3, rots), f32),
            pltpu.VMEM((2 * owners, 2 * CPO, half), bf16),
            pltpu.VMEM((sharers, slots, dev_images), f32),
            pltpu.VMEM((1, dirs), f32),
            pltpu.VMEM((ORDER, dirs), f32),
            pltpu.VMEM((ORDER, dirs), f32),
            pltpu.VMEM((ROWS, dirs), bf16),
            pltpu.VMEM((dirs, wide), bf16),
            pltpu.VMEM((ROWS, wide), f32),
            pltpu.VMEM((COEF, wide), f32),
            pltpu.VMEM((max(ang_size - 1, 1), owners, rows_out, wide), f32),
            pltpu.VMEM((rows_out, wide), f32),
            pltpu.VMEM((owners, rows_out, wide), bf16),
            pltpu.VMEM((owners, rows_out, wide), bf16),
            dma((7 + columns,)),
            dma((2, others)),
            dma((2, others)),
            dma((2, pieces, others)),
            dma((2, max(sharers - 1, 1))),
            dma((2, max(ang_size - 1, 1), owners)),
            dma((2, owners)),
        ],
        compiler_params=pltpu.CompilerParams(
            collective_id=0, has_side_effects=True, vmem_limit_bytes=60 * 1024 * 1024
        ),
    )(
        images.reshape(features, dev_images),
        references.reshape(features, rots),
        noise_weight[None, :],
        candidate_count,
        candidate_rotation,
        euler_angles,
        image_order[None, :],
        jnp.asarray(table),
    )
    coefficients = jnp.transpose(result[:cs, :rows_out]).reshape(rows_out, 2, shells)
    evidence = result[wide : wide + columns, :LANES].reshape(dev_images)
    return (coefficients, evidence)


def solution(mesh):
    in_specs = (
        P(None, "shell", "ang", ("grp", "rot")),
        P(None, "shell", "ang", ("grp", "rot")),
        P(("grp", "shell")),
        P(None, ("grp", "rot")),
        P(("grp", "rot"), None),
        P(("grp", "rot"), None, None),
        P(("grp", "rot")),
    )
    out_specs = (P(("grp", "rot", "ang"), None, "shell"), P(("grp", "rot")))
    return jax.shard_map(
        per_device, mesh=mesh, in_specs=in_specs, out_specs=out_specs, check_vma=False
    )
```

time: 40.3 us -> 31.3 us (0.78)
  local copies, waits for them, and re-layouts: 7.84 us -> 2.71 us
  Pallas kernels: 30.1 us -> 27.8 us
  other arithmetic: 1.33 us -> 0 us
    broadcast_in_dim x5 -> x0, local copies, waits for them, and re-layouts: 3.51 us -> none  [the longest x1 0.74 us: per_device(): jnp.concatenate([noise_weight, noise_weight])[:, None]]
    pallas_call x1, Pallas kernels: 30.1 us -> 27.8 us  [per_device(): pl.pallas_call(functools.partial(kernel, sizes, diagonal), out_shape=jax....]
    pallas_call x1 -> x0, local copies, waits for them, and re-layouts: 1.57 us -> none  [per_device(): pl.pallas_call(functools.partial(kernel, sizes, diagonal), out_shape=(jax...]
    slice x0 -> x1, local copies, waits for them, and re-layouts: none -> 1.47 us  [per_device(): result[:cs, :rows_out]]
    unnamed x1 -> x0, local copies, waits for them, and re-layouts: 1.24 us -> none
    reshape x0 -> x1, local copies, waits for them, and re-layouts: none -> 1.24 us  [per_device(): evidence = result[wide:wide + columns, :LANES].reshape(dev_images)]
    broadcast_in_dim x1 -> x0, other arithmetic: 0.81 us -> none  [per_device(): jnp.concatenate([noise_weight, noise_weight])[:, None]]
    lt x1 -> x0, local copies, waits for them, and re-layouts: 0.76 us -> none  [per_device(): inside = (local >= 0) & (local < count)]
where the time goes in v2:
time: 31.3 us; the launch traced here: 31.1 us
  Pallas kernels  27.8 us (89%)
  local copies, waits for them, and re-layouts  2.71 us (9%)
  between operations  0.64 us (2%)
    pallas_call x1, Pallas kernels, per_device(): pl.pallas_call(functools.partial(kernel, sizes, diagonal), out_shape=jax....  27.8 us
    slice x1, local copies, waits for them, and re-layouts, per_device(): result[:cs, :rows_out]  1.47 us
    reshape x1, local copies, waits for them, and re-layouts, per_device(): evidence = result[wide:wide + columns, :LANES].reshape(dev_images)  1.24 us

profile of v2, /device:TPU:0, one launch (start us, length us, event | category | flops | bytes accessed | tf_op | source)
XLA Modules:
  0.0 31.1 jit_solution(5061110742502843087)
XLA Ops:
  0.6 27.8 %shard_map.95 = f32[136,128]{1,0:T(8,128)} custom-call(f32[4096,256]{1,0:T(8,128)} %bitcast.9, bf16[4096,256]{1,0:T(8,128)(2,1)} %bitcast.10, f32[1,64]{1,0:T(1,128)} %bitcast.13, s32[2,4]{1,0:T(2,128)} %count_in.1, s32[2,4,8]{2,1,0:T(4,128)} %rotation_in.1, f32[3,256]{1,0:T(4,128)} %euler_in.1, s32[1,256]{1,0:T(1,128)} %bitcast.12, ...), custom_call_target="tpu_custom_call" | custom-call | tf_op jit(solution)/shard_map/pallas_call | solution.py:493
  28.4 1.2 %slice_bitcast_fusion = f32[256]{0:T(256)} fusion(f32[136,128]{1,0:T(8,128)} %shard_map.95), kind=kLoop, calls=%fused_computation | loop fusion | bytes 2048 | tf_op jit(solution)/shard_map/reshape | solution.py:549
  29.6 1.5 %slice.6 = f32[128,128]{1,0:T(8,128)} slice(f32[136,128]{1,0:T(8,128)} %shard_map.95), slice={[0:128], [0:128]} | slice | bytes 131072 | tf_op jit(solution)/shard_map/slice | solution.py:548

commit v3 on v2

--- a/solution.py
+++ b/solution.py
@@ -63,6 +63,7 @@
     order_in,
     constants_in,
     out,
+    evidence_out,
     image_buf,
     ref_buf,
     native,
@@ -131,7 +132,8 @@
     for h in range(columns):
         load(images.at[:, h * LANES : (h + 1) * LANES], image_buf.at[h])
 
-    rot_ids = [{"rot": lax.rem(rot + k, owners)} for k in range(1, owners)]
+    hops = sorted(range(1, owners), key=lambda k: abs(2 * k - owners))
+    rot_ids = [{"rot": lax.rem(rot + k, owners)} for k in hops]
     share_ids = []
     for k in range(1, sharers):
         other = lax.rem(lin + k, sharers)
@@ -246,17 +248,6 @@
         moving.append(line)
     slices[owners + rot] = slices[rot]
 
-    for a in range(angles):
-        for part in range(2):
-            for h in range(columns):
-                by_angle[
-                    a * cs + part * shells : a * cs + (part + 1) * shells,
-                    h * LANES : (h + 1) * LANES,
-                ] = (
-                    image_buf[h, pl.ds(part * half + a, shells, stride=angles), :]
-                    * weight_tile[...]
-                ).astype(jnp.bfloat16)
-
     loads[4].wait()
     member = order[...] == lax.broadcasted_iota(jnp.int32, (dev_images, dev_images), 0)
     member = member.astype(jnp.float32).astype(jnp.bfloat16)
@@ -284,9 +275,10 @@
             )
             rows3[i] += jnp.sum(jnp.where(here, value, 0.0), axis=0, keepdims=True)
     phase = (2.0 * math.pi / ANGLES) * angle + rows3[2]
-    cos_p, sin_p = jnp.cos(phase), jnp.sin(phase)
-    cos_a, sin_a = jnp.cos(rows3[0]), jnp.sin(rows3[0])
-    cos_b, sin_b = jnp.cos(rows3[1]), jnp.sin(rows3[1])
+    stacked = jnp.concatenate([rows3[0], rows3[1], phase], axis=0)
+    cosines, sines = jnp.cos(stacked), jnp.sin(stacked)
+    cos_a, cos_b, cos_p = cosines[0:1], cosines[1:2], cosines[2:3]
+    sin_a, sin_b, sin_p = sines[0:1], sines[1:2], sines[2:3]
     x = cos_a * cos_b * cos_p - sin_a * sin_p
     y = sin_a * cos_b * cos_p + cos_a * sin_p
     dir_rows[...] = -sin_b * cos_p
@@ -346,6 +338,17 @@
         moving.append(
             send(shares.at[lin], shares.at[lin], (share_sem.at[0, k], share_sem.at[1, k]), device)
         )
+    for a in range(angles):
+        for part in range(2):
+            for h in range(columns):
+                by_angle[
+                    a * cs + part * shells : a * cs + (part + 1) * shells,
+                    h * LANES : (h + 1) * LANES,
+                ] = (
+                    image_buf[h, pl.ds(part * half + a, shells, stride=angles), :]
+                    * weight_tile[...]
+                ).astype(jnp.bfloat16)
+
     for copy in moving:
         copy.wait_recv()
     sent += moving
@@ -358,14 +361,16 @@
     highest = jnp.max(masked, axis=0, keepdims=True)
     total = jnp.sum(jnp.where(valid, jnp.exp(masked - highest), 0.0), axis=0, keepdims=True)
     evidence = highest + jnp.log(total)
+    evidence_out[...] = evidence
     weights = jnp.where(valid, jnp.exp(masked - evidence), 0.0).astype(jnp.bfloat16)
 
     if cs < averages.shape[1]:
         averages[...] = jnp.zeros(averages.shape, jnp.bfloat16)
-    for a in range(angles):
-        averages[a * slots : (a + 1) * slots, :cs] = nt_dot(
-            weights, by_angle[a * cs : (a + 1) * cs, :]
-        ).astype(jnp.bfloat16)
+    per = 2 if cs % LANES == 0 and angles % 2 == 0 else 1
+    for a in range(0, angles, per):
+        pair = nt_dot(weights, by_angle[a * cs : (a + per) * cs, :]).astype(jnp.bfloat16)
+        for i in range(per):
+            averages[(a + i) * slots : (a + i + 1) * slots, :cs] = pair[:, i * cs : (i + 1) * cs]
 
     def out_rows(rot_id, ang_id):
         return pl.ds(pl.multiple_of((rot_id * ang_size + ang_id) * rows_out, rows_out), rows_out)
@@ -446,10 +451,7 @@
             device_id_type=MESH,
         ).wait_recv()
         total_here = total_here + rot_recv[source].astype(jnp.float32)
-    out[0 : total_here.shape[1], 0:rows_out] = jnp.transpose(total_here)
-    for h in range(columns):
-        row = total_here.shape[1] + h
-        out[row : row + 1, 0:LANES] = evidence[:, h * LANES : (h + 1) * LANES]
+    out[...] = jnp.transpose(total_here)[:cs]
     for copy in sent:
         copy.wait_send()
     for line in across:
@@ -460,6 +462,15 @@
         @pl.when(rot != j)
         def _():
             toward(j).wait_send()
+
+
+def hand_over(coef_in, evidence_in, coef_out, evidence_out, sems):
+    first = pltpu.make_async_copy(coef_in, coef_out, sems.at[0])
+    second = pltpu.make_async_copy(evidence_in, evidence_out, sems.at[1])
+    first.start()
+    second.start()
+    first.wait()
+    second.wait()
 
 
 def per_device(
@@ -485,16 +496,18 @@
     sizes = (owners, shell_size, ang_size, shells, angles, rots)
     f32, bf16 = jnp.float32, jnp.bfloat16
     dma = pltpu.SemaphoreType.DMA
-    out_lanes = max(rows_out, LANES)
     columns = dev_images // LANES
     blocks = candidate_count.shape[0]
     others = max(owners - 1, 1)
     pieces = half // min(half, 1024)
-    result = pl.pallas_call(
+    coefficients, evidence = pl.pallas_call(
         functools.partial(kernel, sizes, diagonal),
-        out_shape=jax.ShapeDtypeStruct((wide + 8, out_lanes), f32),
+        out_shape=(
+            jax.ShapeDtypeStruct((cs, rows_out), f32),
+            jax.ShapeDtypeStruct((1, dev_images), f32),
+        ),
         in_specs=[hbm] * 8,
-        out_specs=vmem,
+        out_specs=(vmem, vmem),
         scratch_shapes=[
             pltpu.VMEM((columns, features, LANES), f32),
             pltpu.VMEM((features, rots), bf16),
@@ -545,9 +558,19 @@
         image_order[None, :],
         jnp.asarray(table),
     )
-    coefficients = jnp.transpose(result[:cs, :rows_out]).reshape(rows_out, 2, shells)
-    evidence = result[wide : wide + columns, :LANES].reshape(dev_images)
-    return (coefficients, evidence)
+    coefficients, evidence = pl.pallas_call(
+        hand_over,
+        out_shape=(
+            jax.ShapeDtypeStruct(coefficients.shape, f32),
+            jax.ShapeDtypeStruct(evidence.shape, f32),
+        ),
+        in_specs=[hbm, hbm],
+        out_specs=(hbm, hbm),
+        scratch_shapes=[dma((2,))],
+        compiler_params=pltpu.CompilerParams(vmem_limit_bytes=60 * 1024 * 1024),
+    )(coefficients, evidence)
+    coefficients = jnp.transpose(coefficients).reshape(rows_out, 2, shells)
+    return (coefficients, evidence.reshape(dev_images))
 
 
 def solution(mesh):

time: 31.3 us -> 30.7 us (0.981); the launches traced: 31.1 us -> 30.2 us
  local copies, waits for them, and re-layouts: 2.71 us -> 0 us
  Pallas kernels: 27.8 us -> 29.6 us
    pallas_call x1 -> x2, Pallas kernels: 27.8 us -> 29.6 us  [the longest x1 26.4 us: per_device(): pl.pallas_call(functools.partial(kernel, sizes, diagonal), out_shape=(jax...]
    slice x1 -> x0, local copies, waits for them, and re-layouts: 1.47 us -> none  [per_device(): result[:cs, :rows_out]]
    reshape x1 -> x0, local copies, waits for them, and re-layouts: 1.24 us -> none  [per_device(): evidence = result[wide:wide + columns, :LANES].reshape(dev_images)]
where the time goes in v3:
time: 30.7 us; the launch traced here: 30.2 us
  Pallas kernels  29.6 us (96%)
  between operations  0.64 us (2%)
    pallas_call x1, Pallas kernels, per_device(): pl.pallas_call(functools.partial(kernel, sizes, diagonal), out_shape=(jax...  26.4 us
    pallas_call x1, Pallas kernels, per_device(): pl.pallas_call(hand_over, out_shape=(jax.ShapeDtypeStruct(coefficients.sh...  3.14 us

profile of v3, /device:TPU:0, one launch (start us, length us, event | category | flops | bytes accessed | tf_op | source)
XLA Modules:
  0.0 30.2 jit_solution(16929221900066737295)
XLA Ops:
  0.6 26.4 %shard_map.95 = (f32[128,128]{1,0:T(8,128)}, f32[1,256]{1,0:T(1,128)}) custom-call(f32[4096,256]{1,0:T(8,128)} %bitcast.8, bf16[4096,256]{1,0:T(8,128)(2,1)} %bitcast.9, f32[1,64]{1,0:T(1,128)} %bitcast.11, s32[2,4]{1,0:T(2,128)} %count_in.1, s32[2,4,8]{2,1,0:T(4,128)} %rotation_in.1, f32[3,256]{1,0:T(4,128)} %euler_in.1, s32[1,256]{1,0:T(1,128)} %bitcast.10, ...), custom_call_target="tpu_custom_call" | custom-call | tf_op jit(solution)/shard_map/pallas_call | solution.py:503
  27.1 3.1 %shard_map.96 = (f32[128,128]{1,0:T(8,128)}, f32[1,256]{1,0:T(1,128)}) custom-call(f32[128,128]{1,0:T(8,128)} %get-tuple-element.6.coef_in, f32[1,256]{1,0:T(1,128)} %get-tuple-element.7.evidence_in), custom_call_target="tpu_custom_call" | custom-call | tf_op jit(solution)/shard_map/pallas_call | solution.py:561

commit v4 on v3

--- a/solution.py
+++ b/solution.py
@@ -15,7 +15,6 @@
 CPO = 8
 COEF = 1024
 HALF = 16
-ROWS = 2 * HALF * HALF + 2 * (ORDER - HALF) * ORDER
 LANES = 128
 CHUNK = 256
 MESH = pl.DeviceIdType.MESH
@@ -37,12 +36,6 @@
             running = running * (2.0 * degree - 1.0) / (2.0 * degree)
         diagonal.append(math.sqrt((2.0 * degree + 1.0) / (4.0 * math.pi) * running))
     return table, diagonal
-
-
-def padded_rows(degree):
-    rows = HALF if degree < HALF else ORDER
-    base = 2 * HALF * min(degree, HALF) + 2 * ORDER * max(degree - HALF, 0)
-    return rows, base
 
 
 def nt_dot(left, right):
@@ -86,10 +79,9 @@
     sin_rows,
     table,
     averages,
-    padded,
+    ordered,
     coef,
     ang_recv,
-    rot_own,
     rot_send,
     rot_recv,
     load_sem,
@@ -214,7 +206,10 @@
                 )
         return carry
 
-    lax.fori_loop(0, shells, weigh, 0, unroll=4)
+    step = min(half, 1024)
+    pieces = half // step
+    early_shells = step // angles
+    lax.fori_loop(0, early_shells, weigh, 0, unroll=4)
 
     for copy in small:
         copy.wait_recv()
@@ -223,8 +218,6 @@
     ids = wanted[...].reshape(slots, LANES)[:, :1]
     selector = (ids == lax.broadcasted_iota(jnp.int32, (slots, rots), 1)).astype(jnp.float32)
     selector = selector.astype(jnp.bfloat16)
-    step = min(half, 1024)
-    pieces = half // step
     moving = []
     for piece in range(pieces):
         start = piece * step
@@ -247,6 +240,7 @@
             )
         moving.append(line)
     slices[owners + rot] = slices[rot]
+    lax.fori_loop(early_shells, shells, weigh, 0, unroll=4)
 
     loads[4].wait()
     member = order[...] == lax.broadcasted_iota(jnp.int32, (dev_images, dev_images), 0)
@@ -287,7 +281,7 @@
     for m in range(ORDER):
         factor = math.sqrt(2.0) if m else 1.0
         cos_rows[m : m + 1, :] = real * factor
-        sin_rows[m : m + 1, :] = imag * factor
+        sin_rows[m : m + 1, :] = imag * factor if m else real
         real, imag = x * real - y * imag, x * imag + y * real
 
     loads[5].wait()
@@ -300,7 +294,7 @@
         prev = jnp.zeros((HALF, width), jnp.float32)
         early = prev
         for degree in range(ORDER):
-            rows, base = padded_rows(degree)
+            rows = HALF if degree < HALF else ORDER
             if degree == HALF:
                 pad = jnp.zeros((ORDER - HALF, width), jnp.float32)
                 prev = jnp.concatenate([prev, pad], axis=0)
@@ -310,11 +304,20 @@
             now = first * (z * prev - second * early)
             azimuth = lax.broadcasted_iota(jnp.int32, (rows, width), 0)
             now = jnp.where(azimuth == degree, diagonal[degree], now)
-            table[base : base + rows, lanes] = (now * cos_rows[:rows, lanes]).astype(jnp.bfloat16)
-            table[base + rows : base + 2 * rows, lanes] = (now * sin_rows[:rows, lanes]).astype(
-                jnp.bfloat16
-            )
+            cosine = now * cos_rows[:rows, lanes]
+            sine = now * sin_rows[:rows, lanes]
+            first_row = degree * degree
+            for h in range(width // LANES):
+                at = slice(h * LANES, (h + 1) * LANES)
+                ordered[h, pl.ds(first_row, degree + 1, stride=2), :] = sine[: degree + 1, at]
+                if degree:
+                    ordered[h, pl.ds(first_row + 1, degree, stride=2), :] = cosine[
+                        1 : degree + 1, at
+                    ]
             prev, early = now, prev
+        for h in range(width // LANES):
+            at = pl.ds(pl.multiple_of(turn * width + h * LANES, LANES), LANES)
+            table[:, at] = ordered[h].astype(jnp.bfloat16)
 
     partial = jnp.zeros((slots, dev_images), jnp.float32)
     for piece in range(pieces):
@@ -372,105 +375,65 @@
         for i in range(per):
             averages[(a + i) * slots : (a + i + 1) * slots, :cs] = pair[:, i * cs : (i + 1) * cs]
 
-    def out_rows(rot_id, ang_id):
-        return pl.ds(pl.multiple_of((rot_id * ang_size + ang_id) * rows_out, rows_out), rows_out)
-
+    moving = []
     across = []
-
-    def start_across(j):
+    turns = hops + [0]
+
+    def start_along(i):
+        total_here = coef[i, ang]
+        for k, copy in enumerate(across[i]):
+            copy.wait_recv()
+            total_here = total_here + ang_recv[k, i]
+        if i < owners - 1:
+            rot_send[i] = total_here.astype(jnp.bfloat16)
+            moving.append(
+                send(
+                    rot_send.at[i],
+                    rot_recv.at[i],
+                    (rot_sem.at[0, i], rot_sem.at[1, i]),
+                    rot_ids[i],
+                )
+            )
+        return total_here
+
+    group = ang_size * rows_out
+    for i, hop in enumerate(turns):
+        start = pl.multiple_of(lax.rem(rot + hop, owners) * group, group)
+        rows = jnp.dot(
+            table[pl.ds(start, group), :], averages[...], preferred_element_type=jnp.float32
+        )
+        for k in range(ang_size):
+            coef[i, k] = rows[k * rows_out : (k + 1) * rows_out]
         line = []
         for k in range(1, ang_size):
             other = lax.rem(ang + k, ang_size)
             line.append(
                 send(
-                    coef.at[out_rows(j, other)],
-                    ang_recv.at[k - 1, j],
-                    (ang_sem.at[0, k - 1, j], ang_sem.at[1, k - 1, j]),
+                    coef.at[i, other],
+                    ang_recv.at[k - 1, i],
+                    (ang_sem.at[0, k - 1, i], ang_sem.at[1, k - 1, i]),
                     {"ang": other},
                 )
             )
         across.append(line)
-
-    def toward(j):
-        return pltpu.make_async_remote_copy(
-            src_ref=rot_send.at[j],
-            dst_ref=rot_recv.at[rot],
-            send_sem=rot_sem.at[0, j],
-            recv_sem=rot_sem.at[1, rot],
-            device_id={"rot": j},
-            device_id_type=MESH,
-        )
-
-    def start_along(j):
-        total_here = coef[out_rows(j, ang), :]
-        for k, copy in enumerate(across[j]):
-            copy.wait_recv()
-            total_here = total_here + ang_recv[k, j]
-
-        @pl.when(rot == j)
-        def _():
-            rot_own[...] = total_here
-
-        @pl.when(rot != j)
-        def _():
-            rot_send[j] = total_here.astype(jnp.bfloat16)
-            toward(j).start()
-
-    tile = 256
-    done = 0
-    degree = 0
-    for block in range(ROWS // tile):
-        at = slice(block * tile, (block + 1) * tile)
-        padded[at, :] = jnp.dot(table[at, :], averages[...], preferred_element_type=jnp.float32)
-        while degree < ORDER and sum(padded_rows(degree)) + padded_rows(degree)[0] <= at.stop:
-            rows, base = padded_rows(degree)
-            first = degree * degree
-            coef[first : first + 1, :] = padded[base : base + 1, :]
-            if degree:
-                coef[pl.ds(first + 1, degree, stride=2), :] = padded[base + 1 : base + 1 + degree]
-                coef[pl.ds(first + 2, degree, stride=2), :] = padded[
-                    base + rows + 1 : base + rows + 1 + degree
-                ]
-            degree += 1
-        while done < owners and (done + 1) * ang_size * rows_out <= degree * degree:
-            start_across(done)
-            done += 1
-            if done > 1:
-                start_along(done - 2)
-    start_along(owners - 1)
-
-    total_here = rot_own[...]
-    for k in range(1, owners):
-        source = lax.rem(rot + k, owners)
-        pltpu.make_async_remote_copy(
-            src_ref=rot_send.at[0],
-            dst_ref=rot_recv.at[source],
-            send_sem=rot_sem.at[0, 0],
-            recv_sem=rot_sem.at[1, source],
-            device_id={"rot": source},
-            device_id_type=MESH,
-        ).wait_recv()
-        total_here = total_here + rot_recv[source].astype(jnp.float32)
+        if i:
+            start_along(i - 1)
+    total_here = start_along(owners - 1)
+    for i, copy in enumerate(moving):
+        copy.wait_recv()
+        total_here = total_here + rot_recv[i].astype(jnp.float32)
+    sent += moving
     out[...] = jnp.transpose(total_here)[:cs]
     for copy in sent:
         copy.wait_send()
     for line in across:
         for copy in line:
             copy.wait_send()
-    for j in range(owners):
-
-        @pl.when(rot != j)
-        def _():
-            toward(j).wait_send()
-
-
-def hand_over(coef_in, evidence_in, coef_out, evidence_out, sems):
-    first = pltpu.make_async_copy(coef_in, coef_out, sems.at[0])
-    second = pltpu.make_async_copy(evidence_in, evidence_out, sems.at[1])
-    first.start()
-    second.start()
-    first.wait()
-    second.wait()
+
+
+def hand_over(coef_in, evidence_in, coef_out, evidence_out):
+    coef_out[...] = coef_in[...]
+    evidence_out[...] = evidence_in[...]
 
 
 def per_device(
@@ -529,21 +492,20 @@
             pltpu.VMEM((1, dirs), f32),
             pltpu.VMEM((ORDER, dirs), f32),
             pltpu.VMEM((ORDER, dirs), f32),
-            pltpu.VMEM((ROWS, dirs), bf16),
+            pltpu.VMEM((COEF, dirs), bf16),
             pltpu.VMEM((dirs, wide), bf16),
-            pltpu.VMEM((ROWS, wide), f32),
-            pltpu.VMEM((COEF, wide), f32),
+            pltpu.VMEM((min(CHUNK, dirs) // LANES, COEF, LANES), f32),
+            pltpu.VMEM((owners, ang_size, rows_out, wide), f32),
             pltpu.VMEM((max(ang_size - 1, 1), owners, rows_out, wide), f32),
-            pltpu.VMEM((rows_out, wide), f32),
-            pltpu.VMEM((owners, rows_out, wide), bf16),
-            pltpu.VMEM((owners, rows_out, wide), bf16),
+            pltpu.VMEM((others, rows_out, wide), bf16),
+            pltpu.VMEM((others, rows_out, wide), bf16),
             dma((7 + columns,)),
             dma((2, others)),
             dma((2, others)),
             dma((2, pieces, others)),
             dma((2, max(sharers - 1, 1))),
             dma((2, max(ang_size - 1, 1), owners)),
-            dma((2, owners)),
+            dma((2, others)),
         ],
         compiler_params=pltpu.CompilerParams(
             collective_id=0, has_side_effects=True, vmem_limit_bytes=60 * 1024 * 1024
@@ -564,10 +526,8 @@
             jax.ShapeDtypeStruct(coefficients.shape, f32),
             jax.ShapeDtypeStruct(evidence.shape, f32),
         ),
-        in_specs=[hbm, hbm],
-        out_specs=(hbm, hbm),
-        scratch_shapes=[dma((2,))],
-        compiler_params=pltpu.CompilerParams(vmem_limit_bytes=60 * 1024 * 1024),
+        in_specs=[vmem, vmem],
+        out_specs=(vmem, vmem),
     )(coefficients, evidence)
     coefficients = jnp.transpose(coefficients).reshape(rows_out, 2, shells)
     return (coefficients, evidence.reshape(dev_images))

time: 30.7 us -> 29.3 us (0.954); the launches traced: 30.2 us -> 29.2 us
  Pallas kernels: 29.6 us -> 28.5 us
    pallas_call x1, Pallas kernels: 3.14 us -> 1.48 us  [per_device(): pl.pallas_call(hand_over, out_shape=(jax.ShapeDtypeStruct(coefficients.sh...]
    pallas_call x1, Pallas kernels: 26.4 us -> 27 us  [per_device(): pl.pallas_call(functools.partial(kernel, sizes, diagonal), out_shape=(jax...]
where the time goes in v4:
time: 29.3 us; the launch traced here: 29.2 us
  Pallas kernels  28.5 us (97%)
  between operations  0.64 us (2%)
    pallas_call x1, Pallas kernels, per_device(): pl.pallas_call(functools.partial(kernel, sizes, diagonal), out_shape=(jax...  27 us
    pallas_call x1, Pallas kernels, per_device(): pl.pallas_call(hand_over, out_shape=(jax.ShapeDtypeStruct(coefficients.sh...  1.48 us

profile of v4, /device:TPU:0, one launch (start us, length us, event | category | flops | bytes accessed | tf_op | source)
XLA Modules:
  0.0 29.2 jit_solution(3000974843019625124)
XLA Ops:
  0.6 27.0 %shard_map.95 = (f32[128,128]{1,0:T(8,128)}, f32[1,256]{1,0:T(1,128)}) custom-call(f32[4096,256]{1,0:T(8,128)} %bitcast.8, bf16[4096,256]{1,0:T(8,128)(2,1)} %bitcast.9, f32[1,64]{1,0:T(1,128)} %bitcast.11, s32[2,4]{1,0:T(2,128)} %count_in.1, s32[2,4,8]{2,1,0:T(4,128)} %rotation_in.1, f32[3,256]{1,0:T(4,128)} %euler_in.1, s32[1,256]{1,0:T(1,128)} %bitcast.10, ...), custom_call_target="tpu_custom_call" | custom-call | tf_op jit(solution)/shard_map/pallas_call | solution.py:466
  27.7 1.5 %shard_map.96 = (f32[128,128]{1,0:T(8,128)}, f32[1,256]{1,0:T(1,128)}) custom-call(f32[128,128]{1,0:T(8,128)} %get-tuple-element.6.coef_in, f32[1,256]{1,0:T(1,128)} %get-tuple-element.7.evidence_in), custom_call_target="tpu_custom_call" | custom-call | tf_op jit(solution)/shard_map/pallas_call | solution.py:523

commit v5 on v4

--- a/solution.py
+++ b/solution.py
@@ -48,6 +48,7 @@
     sizes,
     diagonal,
     images,
+    images_again,
     references,
     weight_in,
     count_in,
@@ -58,6 +59,7 @@
     out,
     evidence_out,
     image_buf,
+    angle_buf,
     ref_buf,
     native,
     by_angle,
@@ -91,6 +93,7 @@
     share_sem,
     ang_sem,
     rot_sem,
+    turn_sem,
 ):
     owners, shell_size, ang_size, shells, angles, rots = sizes
     half = shells * angles
@@ -206,7 +209,7 @@
                 )
         return carry
 
-    step = min(half, 1024)
+    step = min(half, 512)
     pieces = half // step
     early_shells = step // angles
     lax.fori_loop(0, early_shells, weigh, 0, unroll=4)
@@ -240,6 +243,14 @@
             )
         moving.append(line)
     slices[owners + rot] = slices[rot]
+
+    by_turn = []
+    for a in range(angles):
+        by_turn.append(
+            pltpu.make_async_copy(images_again.at[:, a], angle_buf.at[a], turn_sem.at[a])
+        )
+        by_turn[-1].start()
+
     lax.fori_loop(early_shells, shells, weigh, 0, unroll=4)
 
     loads[4].wait()
@@ -341,17 +352,16 @@
         moving.append(
             send(shares.at[lin], shares.at[lin], (share_sem.at[0, k], share_sem.at[1, k]), device)
         )
+    for copy in by_turn:
+        copy.wait()
     for a in range(angles):
         for part in range(2):
             for h in range(columns):
-                by_angle[
-                    a * cs + part * shells : a * cs + (part + 1) * shells,
-                    h * LANES : (h + 1) * LANES,
-                ] = (
-                    image_buf[h, pl.ds(part * half + a, shells, stride=angles), :]
-                    * weight_tile[...]
+                at = slice(h * LANES, (h + 1) * LANES)
+                first = a * cs + part * shells
+                by_angle[first : first + shells, at] = (
+                    angle_buf[a, part * shells : (part + 1) * shells, at] * weight_tile[...]
                 ).astype(jnp.bfloat16)
-
     for copy in moving:
         copy.wait_recv()
     sent += moving
@@ -462,17 +472,18 @@
     columns = dev_images // LANES
     blocks = candidate_count.shape[0]
     others = max(owners - 1, 1)
-    pieces = half // min(half, 1024)
+    pieces = half // min(half, 512)
     coefficients, evidence = pl.pallas_call(
         functools.partial(kernel, sizes, diagonal),
         out_shape=(
             jax.ShapeDtypeStruct((cs, rows_out), f32),
             jax.ShapeDtypeStruct((1, dev_images), f32),
         ),
-        in_specs=[hbm] * 8,
+        in_specs=[hbm] * 9,
         out_specs=(vmem, vmem),
         scratch_shapes=[
             pltpu.VMEM((columns, features, LANES), f32),
+            pltpu.VMEM((angles, cs, dev_images), f32),
             pltpu.VMEM((features, rots), bf16),
             pltpu.VMEM((features, dev_images), bf16),
             pltpu.VMEM((features, dev_images), bf16),
@@ -506,12 +517,14 @@
             dma((2, max(sharers - 1, 1))),
             dma((2, max(ang_size - 1, 1), owners)),
             dma((2, others)),
+            dma((angles,)),
         ],
         compiler_params=pltpu.CompilerParams(
             collective_id=0, has_side_effects=True, vmem_limit_bytes=60 * 1024 * 1024
         ),
     )(
         images.reshape(features, dev_images),
+        images.reshape(cs, angles, dev_images),
         references.reshape(features, rots),
         noise_weight[None, :],
         candidate_count,

time: 29.3 us -> 28.8 us (0.983)
  Pallas kernels: 28.5 us -> 28 us
    pallas_call x1, Pallas kernels: 27 us -> 26.5 us  [per_device(): pl.pallas_call(functools.partial(kernel, sizes, diagonal), out_shape=(jax...]
where the time goes in v5:
time: 28.8 us; the launch traced here: 28.7 us
  Pallas kernels  28 us (97%)
  between operations  0.64 us (2%)
    pallas_call x1, Pallas kernels, per_device(): pl.pallas_call(functools.partial(kernel, sizes, diagonal), out_shape=(jax...  26.5 us
    pallas_call x1, Pallas kernels, per_device(): pl.pallas_call(hand_over, out_shape=(jax.ShapeDtypeStruct(coefficients.sh...  1.48 us

profile of v5, /device:TPU:0, one launch (start us, length us, event | category | flops | bytes accessed | tf_op | source)
XLA Modules:
  0.0 28.7 jit_solution(9017161045302091153)
XLA Ops:
  0.6 26.5 %shard_map.95 = (f32[128,128]{1,0:T(8,128)}, f32[1,256]{1,0:T(1,128)}) custom-call(f32[4096,256]{1,0:T(8,128)} %bitcast.9, f32[128,32,256]{2,1,0:T(8,128)} %bitcast.10, bf16[4096,256]{1,0:T(8,128)(2,1)} %bitcast.11, f32[1,64]{1,0:T(1,128)} %bitcast.13, s32[2,4]{1,0:T(2,128)} %count_in.1, s32[2,4,8]{2,1,0:T(4,128)} %rotation_in.1, f32[3,256]{1,0:T(4,128)} %euler_in.1, ...), custom_call_target="tpu_custom_call" | custom-call | tf_op jit(solution)/shard_map/pallas_call | solution.py:476
  27.2 1.5 %shard_map.96 = (f32[128,128]{1,0:T(8,128)}, f32[1,256]{1,0:T(1,128)}) custom-call(f32[128,128]{1,0:T(8,128)} %get-tuple-element.6.coef_in, f32[1,256]{1,0:T(1,128)} %get-tuple-element.7.evidence_in), custom_call_target="tpu_custom_call" | custom-call | tf_op jit(solution)/shard_map/pallas_call | solution.py:536
